TPU v7x, 32 devices: a whole 2x2x4 slice. The times are simulated.
32 devices in a mesh: dp: 2 (over x), ctx: 16 (over z, y, core).
Axes of the slice: x: 2, y: 2, z: 4, core: 2. Of those that a mesh axis runs over, the one named last changes fastest.
Arguments:
- hidden_in: bfloat16 [2, 2048, 2048], P('dp', 'ctx'), may hold values from -6 to 6
- qk_weight: bfloat16 [2048, 256], replicated, may hold values from -0.125 to 0.125
- conv_weight: float32 [3, 256], replicated, may hold values from -3 to 3
- values: bfloat16 [2, 2048, 512], P('dp', 'ctx'), may hold values from -6 to 6
- gate_in: bfloat16 [2, 2048, 512], P('dp', 'ctx'), may hold values from -6 to 6
- cotangent: bfloat16 [2, 2048, 512], P('dp', 'ctx'), may hold values from -6 to 6
Outputs:
- output: bfloat16 [2, 2048, 512], P('dp', 'ctx')
- grad_hidden: bfloat16 [2, 2048, 2048], P('dp', 'ctx')
- grad_values: bfloat16 [2, 2048, 512], P('dp', 'ctx')
- grad_gate: bfloat16 [2, 2048, 512], P('dp', 'ctx')
- grad_qk_weight: bfloat16 [2048, 256], replicated
All inputs are finite; a program needn't handle non-finite values.
Results may differ from a plain program's by a relative error of at most 0.008.
Values may be sent and summed in bfloat16 or wider, within the bound.
A program may use at most 192 MiB of HBM per device.

v0:
```python
import math

import jax
import jax.numpy as jnp
import numpy as np
from jax import lax
from jax.sharding import PartitionSpec as P

H = 8
F = 16
DV = 64
KCONV = 3


def shifted(array, axis, by):
    length = lax.axis_size(axis)
    pairs = [(i, i + by) for i in range(length) if 0 <= i + by < length]
    return lax.ppermute(array, axis, pairs)


def entering(part, axis, combine, identity):
    place = lax.axis_index(axis)
    gathered = jax.tree.map(lambda a: lax.all_gather(a, axis), part)
    state = jax.tree.map(lambda a, e: jnp.zeros_like(a) + jnp.asarray(e, a.dtype), part, identity)

    def one(hop, state):
        return combine(
            state, jax.tree.map(lambda a: lax.dynamic_index_in_dim(a, hop, 0, False), gathered)
        )

    return lax.fori_loop(0, place, one, state)


def entering_2(array, axis, combine, identity):
    length, here = (lax.axis_size(axis), lax.axis_index(axis))
    everything = jax.tree.map(
        lambda part, kind: lax.all_gather(part.astype(kind), axis),
        array,
        jax.tree.map(lambda a: jnp.bfloat16 if a.dtype == jnp.float32 else a.dtype, array),
    )
    start = jax.tree.map(
        lambda part, zero: jnp.broadcast_to(jnp.asarray(zero, part.dtype), part.shape),
        array,
        identity,
    )

    def hop(k, before):
        at = length - 1 - k
        reached = at > here
        new = combine(
            before, jax.tree.map(lambda part, own: part[at].astype(own.dtype), everything, array)
        )
        return jax.tree.map(lambda a, b: jnp.where(reached, a, b), new, before)

    return lax.fori_loop(0, length, hop, start)


def pair_table(feat_width):
    table = np.zeros((feat_width * feat_width, feat_width * (feat_width + 1) // 2), np.float32)
    column = 0
    for first in range(feat_width):
        for second in range(first, feat_width):
            factor = 1.0 / math.sqrt(feat_width)
            if first == second:
                factor = factor / math.sqrt(2.0)
            table[first * feat_width + second, column] = factor
            column += 1
    return table


def taylor_map(matrix):
    feat_width = matrix.shape[-1]
    outer = (matrix[..., :, None] * matrix[..., None, :]).reshape(
        matrix.shape[:-1] + (feat_width * feat_width,)
    )
    second = jnp.dot(outer, pair_table(feat_width), precision=lax.Precision.HIGHEST)
    ones = jnp.ones(matrix.shape[:-1] + (1,), matrix.dtype)
    return jnp.concatenate([ones, matrix * feat_width ** (-0.25), second], -1)


def add_states(earlier, later):
    return jax.tree.map(jnp.add, earlier, later)


def body(hidden_in, qk_weight, conv_weight, values, gate_in, cotangent):
    highest_precision = lax.Precision.HIGHEST
    tokens = hidden_in[0]
    length = tokens.shape[0]
    half_width = qk_weight.shape[1] // 2
    projected = jnp.dot(tokens, qk_weight, preferred_element_type=jnp.float32).astype(jnp.bfloat16)
    earlier_rows = shifted(projected[length - (KCONV - 1) :], "ctx", 1)
    padded = jnp.concatenate([earlier_rows, projected], 0).astype(jnp.float32)
    mixed = conv_weight[0] * padded[KCONV - 1 : KCONV - 1 + length]
    for offset in range(1, KCONV):
        mixed = (
            mixed + conv_weight[offset] * padded[KCONV - 1 - offset : KCONV - 1 - offset + length]
        )
    queries = mixed[:, :half_width].reshape(length, H, F)
    keys_mat = mixed[:, half_width:].reshape(length, H, F)
    value_matrix = values[0].astype(jnp.float32).reshape(length, H, DV)
    query_feature_rows = taylor_map(queries)
    key_feature_rows = taylor_map(keys_mat)
    scores = jnp.einsum("thf,shf->hts", queries, keys_mat, precision=highest_precision) * F ** (
        -0.5
    )
    rows_idx = lax.broadcasted_iota(jnp.int32, (length, length), 0)
    cols_idx = lax.broadcasted_iota(jnp.int32, (length, length), 1)
    causal = (rows_idx >= cols_idx)[None]
    weights_mat = jnp.where(causal, 1.0 + scores + 0.5 * scores * scores, 0.0)
    local_numerator = jnp.einsum(
        "hts,shd->thd", weights_mat, value_matrix, precision=highest_precision
    )
    denom_local = jnp.sum(weights_mat, 2).T
    own_numerator = jnp.einsum(
        "oxa,oxn->xan", key_feature_rows, value_matrix, precision=highest_precision
    )
    norm_own = jnp.sum(key_feature_rows, 0)
    gate_f = gate_in[0].astype(jnp.float32)
    sigm = jax.nn.sigmoid(gate_f)
    gate_act = gate_f * sigm
    upstream = cotangent[0].astype(jnp.float32)
    grad_attended = (upstream * gate_act).reshape(length, H, DV)
    incoming_numerator, norm_in = entering(
        (own_numerator, norm_own),
        "ctx",
        add_states,
        (jnp.zeros_like(own_numerator), jnp.zeros_like(norm_own)),
    )
    denom = denom_local + jnp.einsum(
        "thm,hm->th", query_feature_rows, norm_in, precision=highest_precision
    )
    numerator_gradient = grad_attended / denom[..., None]
    attended = (
        local_numerator
        + jnp.einsum(
            "jfn,fna->jfa", query_feature_rows, incoming_numerator, precision=highest_precision
        )
    ) / denom[..., None]
    grad_denom = -jnp.sum(grad_attended * attended, -1) / denom
    incoming_numerator_gradient = jnp.einsum(
        "oxa,oxn->xan", query_feature_rows, numerator_gradient, precision=highest_precision
    )
    grad_norm_in = jnp.einsum(
        "thm,th->hm", query_feature_rows, grad_denom, precision=highest_precision
    )
    numerator_following, norm_following = entering_2(
        (incoming_numerator_gradient, grad_norm_in),
        "ctx",
        add_states,
        (jnp.zeros_like(incoming_numerator_gradient), jnp.zeros_like(grad_norm_in)),
    )
    attended_flat = attended.reshape(length, H * DV)
    output = (attended_flat * gate_act).astype(jnp.bfloat16)
    grad_gate = (upstream * attended_flat * sigm * (1.0 + gate_f * (1.0 - sigm))).astype(
        jnp.bfloat16
    )
    grad_weights = (
        jnp.einsum("thd,shd->hts", numerator_gradient, value_matrix, precision=highest_precision)
        + grad_denom.T[:, :, None]
    )
    grad_scores = jnp.where(causal, grad_weights * (1.0 + scores), 0.0) * F ** (-0.5)
    grad_query = jnp.einsum("hts,shf->thf", grad_scores, keys_mat, precision=highest_precision)
    grad_key = jnp.einsum("hts,thf->shf", grad_scores, queries, precision=highest_precision)
    value_gradient_rows = jnp.einsum(
        "hts,thd->shd", weights_mat, numerator_gradient, precision=highest_precision
    )
    value_gradient_rows = value_gradient_rows + jnp.einsum(
        "jfn,fna->jfa", key_feature_rows, numerator_following, precision=highest_precision
    )
    grad_qfeats = (
        jnp.einsum(
            "gpf,pnf->gpn", numerator_gradient, incoming_numerator, precision=highest_precision
        )
        + grad_denom[..., None] * norm_in[None]
    )
    grad_kfeats = (
        jnp.einsum("gpf,pnf->gpn", value_matrix, numerator_following, precision=highest_precision)
        + norm_following[None]
    )
    unused_q, pull_query = jax.vjp(taylor_map, queries)
    unused_k, pull_key = jax.vjp(taylor_map, keys_mat)
    grad_query = grad_query + pull_query(grad_qfeats)[0]
    grad_key = grad_key + pull_key(grad_kfeats)[0]
    grad_values = value_gradient_rows.reshape(length, H * DV).astype(jnp.bfloat16)
    grad_mixed = jnp.concatenate(
        [grad_query.reshape(length, half_width), grad_key.reshape(length, half_width)], 1
    )
    later_rows = shifted(grad_mixed[: KCONV - 1], "ctx", -1)
    extended = jnp.concatenate([grad_mixed, later_rows], 0)
    grad_projected = conv_weight[0] * extended[0:length]
    for offset in range(1, KCONV):
        grad_projected = grad_projected + conv_weight[offset] * extended[offset : offset + length]
    grad_projected = grad_projected.astype(jnp.bfloat16)
    grad_hidden = jnp.dot(grad_projected, qk_weight.T, preferred_element_type=jnp.float32).astype(
        jnp.bfloat16
    )
    local_term = jnp.einsum("tr,tc->rc", tokens, grad_projected, preferred_element_type=jnp.float32)
    grad_qk_weight = lax.psum(local_term, ("dp", "ctx")).astype(jnp.bfloat16)
    return (output[None], grad_hidden[None], grad_values[None], grad_gate[None], grad_qk_weight)


def solution(mesh):
    return jax.shard_map(
        body,
        mesh=mesh,
        in_specs=(
            P("dp", "ctx", None),
            P(),
            P(),
            P("dp", "ctx", None),
            P("dp", "ctx", None),
            P("dp", "ctx", None),
        ),
        out_specs=(
            P("dp", "ctx", None),
            P("dp", "ctx", None),
            P("dp", "ctx", None),
            P("dp", "ctx", None),
            P(),
        ),
        check_vma=False,
    )
```

profile of v0, /device:TPU:0, one launch (start us, length us, event | category | flops | bytes accessed | tf_op | source)
XLA Modules:
  0.0 300.4 jit_solution(2663749465147773364)
XLA Ops:
  7.3 1.1 copy-done
  8.4 1.3 convolution_convert_fusion.2
  9.8 2.4 collective-permute-start
  12.9 1.0 copy.76
  15.1 1.7 fusion.19
  19.1 26.0 %all-gather.1 = f32[128,153]{1,0:T(8,128)} all-gather(f32[8,153]{1,0:T(8,128)S(1)} %fusion.18), channel_id=3, replica_groups=mesh['dp'=2,'ctx'=16] {'ctx'}, dimensions={0}, use_global_device_ids=true | all-gather | bytes 83232 | tf_op jit(solution)/shard_map/all_gather | solution.py:23
  45.8 1.8 fusion.22
  47.7 1.5 fusion.50
  49.2 46.4 %all-gather.7.cloned.1.call-done = f32[128,153,64]{1,2,0:T(8,128)} async-done(((f32[8,153,64]{1,2,0:T(8,128)}), f32[128,153,64]{1,2,0:T(8,128)}) %all-gather.7.cloned.1.call-update) | async-done | bytes 5013520 | tf_op jit(solution)/shard_map/all_gather | solution.py:23
  96.0 1.8 fusion.33
  97.8 2.6 convolution_bitcast_fusion.3
  100.4 2.5 multiply_reduce_fusion.4
  102.9 2.2 convolution_convert_fusion.1
  105.1 1.7 fusion.2
  106.9 2.0 fusion.13
  111.1 2.3 fusion.46
  113.3 1.1 copy.82
  114.4 50.1 %all-gather.3 = bf16[128,153]{1,0:T(8,128)(2,1)S(1)} all-gather(bf16[8,153]{1,0:T(8,128)(2,1)S(1)} %bitcast.148), channel_id=5, replica_groups=mesh['dp'=2,'ctx'=16] {'ctx'}, dimensions={0}, use_global_device_ids=true | all-gather | bytes 41616 | tf_op jit(solution)/shard_map/all_gather | solution.py:37
  164.5 1.8 multiply_convert_fusion
  166.3 21.1 %all-gather.9.cloned.1.call-done = bf16[128,153,64]{1,2,0:T(8,128)(2,1)} async-done(((bf16[8,153,64]{1,2,0:T(8,128)(2,1)}), bf16[128,153,64]{1,2,0:T(8,128)(2,1)}) %all-gather.9.cloned.1.call-update) | async-done | bytes 2506768 | tf_op jit(solution)/shard_map/all_gather | solution.py:37
  187.4 25.5 %while.31 = (s32[]{:T(128)}, f32[8,153,64]{2,1,0:T(8,128)S(1)}, f32[8,153]{1,0:T(8,128)S(1)}, s32[]{:T(128)}, bf16[16,8,153,64]{2,3,1,0:T(8,128)(2,1)}, /*index=...) while((s32[]{:T(128)}, f32[8,153,64]{2,1,0:T(8,128)S(1)}, ...), condition=%wide.region_8.9_spmd.clone, body=%wide.region_7.8_spmd.clone.sunk | while | flops 318248 | bytes 1422465 | solution.py:55
  195.4 1.0 constant_dynamic-slice_fusion.5
  205.0 1.0 constant_dynamic-slice_fusion.5
  212.9 2.4 fusion.17
  215.4 1.4 fusion.1
  216.8 2.0 fusion.11
  220.2 1.3 collective-permute-start.1
  221.5 1.1 fusion.8
  223.5 1.5 convolution_bitcast_fusion
  225.0 1.3 fusion
  226.3 65.0 %all-reduce.1 = bf16[2048,256]{0,1:T(8,128)(2,1)} all-reduce(f32[2048,256]{0,1:T(8,128)S(1)} %convolution_bitcast_fusion), channel_id=1, replica_groups=mesh['dp'=2,'ctx'=16] {'dp','ctx'}, use_global_device_ids=true, to_apply=%region_11.12 | all-reduce | flops 524288 | bytes 3145728 | tf_op jit(solution)/shard_map/psum | solution.py:198
  291.3 2.3 copy.99
  (154 shorter events, 32.5 us)
Async XLA Ops:
  7.2 1.2 copy-start
  7.2 7.2 %copy-start.8 = (f32[256,136,1]{0,1,2:T(8,128)S(1)}, f32[256,136,1]{0,1,2:T(8,128)}, u32[]{:S(2)}) copy-start(f32[256,136,1]{0,1,2:T(8,128)} %constant.82) | copy-start | bytes 417796
  7.2 9.7 %copy-start.17 = (bf16[1,128,512]{2,1,0:T(8,128)(2,1)S(1)}, bf16[1,128,512]{2,1,0:T(8,128)(2,1)}, u32[]{:S(2)}) copy-start(bf16[1,128,512]{2,1,0:T(8,128)(2,1)} %param.19) | copy-start | bytes 393220
  7.2 10.5 %copy-start.18 = (bf16[1,128,512]{2,1,0:T(8,128)(2,1)S(1)}, bf16[1,128,512]{2,1,0:T(8,128)(2,1)}, u32[]{:S(2)}) copy-start(bf16[1,128,512]{2,1,0:T(8,128)(2,1)} %param.18) | copy-start | bytes 393220
  7.2 88.4 %all-gather.7.cloned.1.call-start = ((), (), s32[]{:S(2)}) async-start(), calls=%async_computation | async-start | bytes 8912896 | tf_op jit(solution)/shard_map/all_gather | solution.py:23
  9.8 4.2 %collective-permute-start = (bf16[2,256]{1,0:T(2,128)(2,1)S(1)}, bf16[2,256]{1,0:T(2,128)(2,1)S(1)}, u32[]{:S(2)}, u32[]{:S(2)}) collective-permute-start(bf16[2,256]{1,0:T(2,128)(2,1)S(1)} %slice.51), channel_id=1, source_target_pairs={{0,1},{1,2},{2,3},{3,4},{4,5},{5,6},{6,7},{7,8},{8,9},{9,10},{10,1... | collective-permute-start | bytes 3080 | tf_op jit(solution)/shard_map/ppermute | solution.py:18
  12.9 1.1 copy-start.19
  12.9 1.1 copy-start.21
  12.9 1.1 copy-start.23
  14.0 33.6 %copy-start.11 = (bf16[1,128,512]{1,2,0:T(8,128)(2,1)}, bf16[1,128,512]{1,2,0:T(8,128)(2,1)S(1)}, u32[]{:S(2)}) copy-start(bf16[1,128,512]{1,2,0:T(8,128)(2,1)S(1)} %copy.76) | copy-start | bytes 393220
  14.3 33.4 %copy-start.14 = (f32[128,8,16]{0,2,1:T(8,128)}, f32[128,8,16]{0,2,1:T(8,128)S(1)}, u32[]{:S(2)}) copy-start(f32[128,8,16]{0,2,1:T(8,128)S(1)} %broadcast_multiply_fusion.3) | copy-start | bytes 196612
  16.8 170.6 %all-gather.9.cloned.1.call-start = ((), (), s32[]{:S(2)}) async-start(), calls=%async_computation.1 | async-start | bytes 4456448 | tf_op jit(solution)/shard_map/all_gather | solution.py:37
  18.6 77.1 %copy-start.5 = (f32[128,128]{0,1:T(8,128)}, f32[128,128]{0,1:T(8,128)S(1)}, u32[]{:S(2)}) copy-start(f32[128,128]{0,1:T(8,128)S(1)} %copy.74) | copy-start | bytes 196612
  95.9 6.9 %copy-start.1 = (f32[128,8,136]{0,2,1:T(8,128)S(1)}, f32[128,8,136]{0,2,1:T(8,128)}, u32[]{:S(2)}) copy-start(f32[128,8,136]{0,2,1:T(8,128)} %fusion.50) | copy-start | bytes 1671172
  95.9 6.9 %copy-start.15 = (f32[128,8,16]{0,2,1:T(8,128)S(1)}, f32[128,8,16]{0,2,1:T(8,128)}, u32[]{:S(2)}) copy-start(f32[128,8,16]{0,2,1:T(8,128)} %broadcast_multiply_fusion.2) | copy-start | bytes 196612
  100.4 8.5 %copy-start.6 = (f32[128,128]{0,1:T(8,128)S(1)}, f32[128,128]{0,1:T(8,128)}, u32[]{:S(2)}) copy-start(f32[128,128]{0,1:T(8,128)} %copy-done.5) | copy-start | bytes 196612
  102.8 2.2 copy-start.2
  102.8 6.4 %copy-start.12 = (bf16[1,128,512]{1,2,0:T(8,128)(2,1)S(1)}, bf16[1,128,512]{1,2,0:T(8,128)(2,1)}, u32[]{:S(2)}) copy-start(bf16[1,128,512]{1,2,0:T(8,128)(2,1)} %copy-done.11) | copy-start | bytes 393220
  105.0 6.0 %copy-start.16 = (f32[128,8,16]{0,2,1:T(8,128)S(1)}, f32[128,8,16]{0,2,1:T(8,128)}, u32[]{:S(2)}) copy-start(f32[128,8,16]{0,2,1:T(8,128)} %broadcast_multiply_fusion.2) | copy-start | bytes 196612
  105.1 4.2 %copy-start.3 = (f32[128,8,64]{0,2,1:T(8,128)S(1)}, f32[128,8,64]{0,2,1:T(8,128)}, u32[]{:S(2)}) copy-start(f32[128,8,64]{0,2,1:T(8,128)} %copy-done.2) | copy-start | bytes 786436
  105.1 4.2 %copy-start.9 = (f32[8,128,128]{1,2,0:T(8,128)S(1)}, f32[8,128,128]{1,2,0:T(8,128)}, u32[]{:S(2)}) copy-start(f32[8,128,128]{1,2,0:T(8,128)} %get-tuple-element.308) | copy-start | bytes 1572868
  212.9 6.2 %copy-start.7 = (f32[128,128]{0,1:T(8,128)S(1)}, f32[128,128]{0,1:T(8,128)}, u32[]{:S(2)}) copy-start(f32[128,128]{0,1:T(8,128)} %copy-done.5) | copy-start | bytes 196612
  212.9 7.3 %copy-start.13 = (f32[128,128]{1,0:T(8,128)S(1)}, f32[128,128]{1,0:T(8,128)}, u32[]{:S(2)}) copy-start(f32[128,128]{1,0:T(8,128)} %copy.93) | copy-start | bytes 196612
  212.9 8.6 %copy-start.4 = (f32[128,8,64]{0,2,1:T(8,128)S(1)}, f32[128,8,64]{0,2,1:T(8,128)}, u32[]{:S(2)}) copy-start(f32[128,8,64]{0,2,1:T(8,128)} %copy-done.2) | copy-start | bytes 786436
  215.3 6.2 %copy-start.10 = (f32[8,128,128]{1,2,0:T(8,128)S(1)}, f32[8,128,128]{1,2,0:T(8,128)}, u32[]{:S(2)}) copy-start(f32[8,128,128]{1,2,0:T(8,128)} %get-tuple-element.308) | copy-start | bytes 1572868
  215.3 8.1 %copy-start.20 = (f32[1,256]{1,0:T(1,128)S(1)}, f32[1,256]{1,0:T(1,128)}, u32[]{:S(2)}) copy-start(f32[1,256]{1,0:T(1,128)} %copy-done.19) | copy-start | bytes 3076
  215.4 8.1 %copy-start.22 = (f32[1,256]{1,0:T(1,128)S(1)}, f32[1,256]{1,0:T(1,128)}, u32[]{:S(2)}) copy-start(f32[1,256]{1,0:T(1,128)} %copy-done.21) | copy-start | bytes 3076
  215.4 8.1 %copy-start.24 = (f32[1,256]{1,0:T(1,128)S(1)}, f32[1,256]{1,0:T(1,128)}, u32[]{:S(2)}) copy-start(f32[1,256]{1,0:T(1,128)} %copy-done.23) | copy-start | bytes 3076
  220.2 3.2 %collective-permute-start.1 = (f32[2,256]{1,0:T(2,128)S(1)}, f32[2,256]{1,0:T(2,128)S(1)}, u32[]{:S(2)}, u32[]{:S(2)}) collective-permute-start(f32[2,256]{1,0:T(2,128)S(1)} %fusion.35), channel_id=1, source_target_pairs={{1,0},{2,1},{3,2},{4,3},{5,4},{6,5},{7,6},{8,7},{9,8},{10,9},{11,1... | collective-permute-start | bytes 6152 | tf_op jit(solution)/shard_map/ppermute | solution.py:18
Sparse Core Ops, SparseCore 0:
  17.0 78.6 all-gather.6
  105.2 82.1 all-gather.8
where the time goes:
time: 303 us; the launch traced here: 300 us
  blocking collectives  141 us (47%)
  waiting for transfers between devices  67.5 us (22%)
  matrix products  33.7 us (11%)
  local copies, waits for them, and re-layouts  28.9 us (10%)
  between operations  14.6 us (5%)
  other arithmetic  9.88 us (3%)
  starting transfers between devices  3.73 us (1%)
    psum x1, blocking collectives, body(): grad_qk_weight = lax.psum(local_term, ('dp', 'ctx')).astype(jnp.bfloat16)  65 us
    all_gather x1, blocking collectives, entering_2(): lax.all_gather(part.astype(kind), axis)  50.1 us
    all_gather x1, waiting for transfers between devices, entering(): gathered = jax.tree.map(lambda a: lax.all_gather(a, axis), part)  46.4 us
    all_gather x1, blocking collectives, entering(): gathered = jax.tree.map(lambda a: lax.all_gather(a, axis), part)  26 us
    all_gather x1, waiting for transfers between devices, entering_2(): lax.all_gather(part.astype(kind), axis)  21.1 us
    dynamic_slice x32, local copies, waits for them, and re-layouts, hop(): part[at].astype(own.dtype)  19 us
    dot_general x4, matrix products, taylor_map(): jnp.dot(outer, pair_table(feat_width), precision=lax.Precision.HIGHEST)  6.19 us
  transfers between devices with their start and end apart: 4, of which 2 were waited for; matrix products, arithmetic and copies ran while one was open for 7% of the time, Pallas kernels for 0%

commit v1 on v0

v1 whole, which is shorter than its diff:
```python
import functools

import jax
import jax.numpy as jnp
import numpy as np
from jax import lax
from jax.experimental import pallas as pl
from jax.experimental.pallas import tpu as pltpu
from jax.sharding import PartitionSpec as P

H = 8
F = 16
DV = 64
KCONV = 3
FP = 256
F32 = jnp.float32
BF16 = jnp.bfloat16
MESH = pl.DeviceIdType.MESH
VM = pl.BlockSpec(memory_space=pltpu.VMEM)
NORM_ROW = H * DV + 2 * DV


def feature_tables():
    pairs = [(a, b) for a in range(F + 1) for b in range(a, F + 1)]
    first = np.zeros((H * F, H * FP), np.float32)
    second = np.zeros((H * F, H * FP), np.float32)
    rows = np.zeros((8, H * FP), np.float32)
    for h in range(H):
        for m, (a, b) in enumerate(pairs):
            lane = h * FP + (m if m < 128 else 128 + 32 * (h % 4) + m - 128)
            if a:
                first[h * F + a - 1, lane] = 1.0
            else:
                rows[0, lane] = 1.0
            if b:
                second[h * F + b - 1, lane] = 1.0
            else:
                rows[1, lane] = 1.0
            scale = 1.0 if b == 0 else 1.0 / F**0.5 if a == 0 else 1.0 / F
            rows[2, lane] = scale * (0.5 if a == b and a else 1.0)
    return first, second, rows


def mm(a, b, ca=1, cb=0):
    return lax.dot_general(a, b, (((ca,), (cb,)), ((), ())), preferred_element_type=F32)


def head_slice(array, h):
    return array[:, h * DV : (h + 1) * DV]


def head_state(state, h):
    tail = H * DV + (h // 4) * DV
    return jnp.concatenate(
        [state[h * DV : (h + 1) * DV], state[tail : tail + DV]], 1
    )


def head_norm(norms, h):
    tail = H + h // 4
    return jnp.concatenate([norms[h : h + 1], norms[tail : tail + 1]], 1)


def store_state(ref, states, norms):
    for h in range(H):
        ref[h * DV : (h + 1) * DV, :] = states[h][:, :128].astype(BF16)
    for g in range(2):
        tail = sum(states[4 * g + i][:, 128:] for i in range(4))
        ref[H * DV + g * DV : H * DV + (g + 1) * DV, :] = tail.astype(BF16)
    rows = [norms[h][:, :128] for h in range(H)]
    rows += [sum(norms[4 * g + i][:, 128:] for i in range(4)) for g in range(2)]
    rows.append(jnp.zeros((16 - len(rows), 128), F32))
    ref[NORM_ROW : NORM_ROW + 16, :] = jnp.concatenate(rows, 0).astype(BF16)
    rest = ref.shape[0] - NORM_ROW - 16
    if rest:
        ref[NORM_ROW + 16 :, :] = jnp.zeros((rest, 128), BF16)


def key_kernel(proj, prev, conv, values, first, second, rows, mixed_out, state_out):
    length = proj.shape[0]
    padded = jnp.concatenate([prev[...], proj[...].astype(F32)], 0)
    mixed = conv[0:1, :] * padded[8 : 8 + length]
    for j in range(1, KCONV):
        mixed = mixed + conv[j : j + 1, :] * padded[8 - j : 8 - j + length]
    mixed_out[...] = mixed
    keys = mixed[:, H * F :].astype(BF16)
    states, norms = [], []
    for h in range(H):
        at = slice(h * FP, (h + 1) * FP)
        phi = (mm(keys, first[:, at]) + rows[0:1, at]) * (mm(keys, second[:, at]) + rows[1:2, at])
        states.append(mm(head_slice(values, h), phi.astype(BF16), 0, 0))
        norms.append(jnp.sum(phi, 0, keepdims=True))
    store_state(state_out, states, norms)


def query_kernel(
    mixed, values, gate, cot, state, first, second, rows, out, ggate, state_out, dq_out, dk_out, dv_out
):
    length = mixed.shape[0]
    q = mixed[:, : H * F].astype(BF16)
    k = mixed[:, H * F :].astype(BF16)
    lane = lax.broadcasted_iota(jnp.int32, (length, H * F), 1) // F
    causal = lax.broadcasted_iota(jnp.int32, (length, length), 0) >= lax.broadcasted_iota(
        jnp.int32, (length, length), 1
    )
    zero = jnp.zeros_like(q)
    incoming = state[...]
    norm_rows = incoming[NORM_ROW : NORM_ROW + 16].astype(F32)
    dq = jnp.zeros((length, H * F), F32)
    dk = jnp.zeros((length, H * F), F32)
    states, norms, outs, ggates, dvs = [], [], [], [], []
    for h in range(H):
        at = slice(h * FP, (h + 1) * FP)
        first_h, second_h, scale = first[:, at], second[:, at], rows[2:3, at]
        qh = jnp.where(lane == h, q, zero)
        kh = jnp.where(lane == h, k, zero)
        v = head_slice(values, h)
        s = mm(qh, k, 1, 1) * F**-0.5
        w = jnp.where(causal, 1.0 + s + 0.5 * s * s, 0.0)
        w16 = w.astype(BF16)
        one = mm(q, first_h) + rows[0:1, at]
        two = (mm(q, second_h) + rows[1:2, at]) * scale
        phi = one * two
        phi16 = phi.astype(BF16)
        state_h = head_state(incoming, h)
        norm_h = head_norm(norm_rows, h)
        den = jnp.sum(w, 1, keepdims=True) + jnp.sum(phi * norm_h, 1, keepdims=True)
        inv = 1.0 / den
        att = (mm(w16, v) + mm(phi16, state_h, 1, 1)) * inv
        g = head_slice(gate, h).astype(F32)
        up = head_slice(cot, h).astype(F32)
        sig = 1.0 / (1.0 + jnp.exp(-g))
        act = g * sig
        ga = up * act
        gd = -jnp.sum(ga * att, 1, keepdims=True) * inv
        ng = (ga * inv).astype(BF16)
        outs.append((att * act).astype(BF16))
        ggates.append((up * att * sig * (1.0 + g * (1.0 - sig))).astype(BF16))
        states.append(mm(ng, phi16, 0, 0))
        norms.append(jnp.sum(gd * phi, 0, keepdims=True))
        dw = mm(ng, v, 1, 1) + gd
        ds = (jnp.where(causal, dw * (1.0 + s), 0.0) * F**-0.5).astype(BF16)
        dphi = mm(ng, state_h) + gd * norm_h
        dq = dq + mm(ds, kh)
        dq = dq + mm((dphi * two).astype(BF16), first_h, 1, 1)
        dq = dq + mm((dphi * one * scale).astype(BF16), second_h, 1, 1)
        dk = dk + mm(ds, qh, 0, 0)
        dvs.append(mm(w16, ng, 0, 0))
    for p in range(H // 2):
        at = slice(2 * p * DV, 2 * (p + 1) * DV)
        out[:, at] = jnp.concatenate(outs[2 * p : 2 * p + 2], 1)
        ggate[:, at] = jnp.concatenate(ggates[2 * p : 2 * p + 2], 1)
        dv_out[:, at] = jnp.concatenate(dvs[2 * p : 2 * p + 2], 1)
    store_state(state_out, states, norms)
    dq_out[...] = dq
    dk_out[...] = dk


def value_kernel(mixed, values, state, dq_in, dk_in, dv_in, first, second, rows, gv, gm):
    keys = mixed[:, H * F :].astype(BF16)
    incoming = state[...]
    norm_rows = incoming[NORM_ROW : NORM_ROW + 16].astype(F32)
    dk = dk_in[...]
    dvs = []
    for h in range(H):
        at = slice(h * FP, (h + 1) * FP)
        first_h, second_h = first[:, at], second[:, at]
        one = mm(keys, first_h) + rows[0:1, at]
        two = mm(keys, second_h) + rows[1:2, at]
        state_h = head_state(incoming, h)
        dphi = mm(head_slice(values, h), state_h) + head_norm(norm_rows, h)
        dk = dk + mm((dphi * two).astype(BF16), first_h, 1, 1)
        dk = dk + mm((dphi * one).astype(BF16), second_h, 1, 1)
        dvs.append(mm((one * two).astype(BF16), state_h, 1, 1))
    for p in range(H // 2):
        at = slice(2 * p * DV, 2 * (p + 1) * DV)
        gv[:, at] = (dv_in[:, at] + jnp.concatenate(dvs[2 * p : 2 * p + 2], 1)).astype(BF16)
    gm[:, : H * F] = dq_in[...]
    gm[:, H * F :] = dk


def hidden_kernel(gm, later, conv, weight, gp_out, gh):
    length = gm.shape[0]
    extended = jnp.concatenate([gm[...], later[...]], 0)
    gp = conv[0:1, :] * extended[0:length]
    for j in range(1, KCONV):
        gp = gp + conv[j : j + 1, :] * extended[j : j + length]
    gp = gp.astype(BF16)
    gp_out[...] = gp
    gh[...] = mm(gp, weight[...], 1, 1).astype(BF16)


def scan_kernel(n, backward, state, out, got, sums, send1, recv1, send2, recv2):
    me = lax.axis_index("ctx")
    dp = lax.axis_index("dp")

    def peer(off):
        return lax.rem(me + off, n)

    barrier = pltpu.get_barrier_semaphore()

    def greet(off, c):
        pl.semaphore_signal(barrier, inc=1, device_id=(dp, peer(off)), device_id_type=MESH)
        return c

    lax.fori_loop(1, n, greet, 0)
    pl.semaphore_wait(barrier, n - 1)

    def copy1(off):
        return pltpu.make_async_remote_copy(
            src_ref=state.at[peer(off)], dst_ref=got.at[me], send_sem=send1.at[off],
            recv_sem=recv1.at[off], device_id=(dp, peer(off)), device_id_type=MESH,
        )

    def copy2(off):
        return pltpu.make_async_remote_copy(
            src_ref=sums.at[peer(off)], dst_ref=out.at[me], send_sem=send2.at[off],
            recv_sem=recv2.at[off], device_id=(dp, peer(off)), device_id_type=MESH,
        )

    def each(f):
        def step(off, c):
            f(off)
            return c
        lax.fori_loop(1, n, step, 0)

    each(lambda off: copy1(off).start())
    got[me] = state[me]
    each(lambda off: copy1(off).wait_recv())

    def add(i, total):
        at = n - 1 - i if backward else i
        sums[at] = total.astype(BF16)
        return total + got[at].astype(F32)

    lax.fori_loop(0, n, add, jnp.zeros(got.shape[1:], F32))
    each(lambda off: copy2(off).start())
    out[me] = sums[me]
    each(lambda off: copy2(off).wait_recv())
    each(lambda off: copy1(off).wait_send())
    each(lambda off: copy2(off).wait_send())


def weight_kernel(n, dps, gp, hidden, out, gps, hid, part, got, sa, ra, sb, rb, sc, rc, sd, rd, se, re):
    dp, me = lax.axis_index("dp"), lax.axis_index("ctx")
    half = n // 2
    core, place = lax.rem(me, 2), me // 2
    own = dp * 2 + core
    team = dps * 2
    width = hidden.shape[1] // team
    tokens = hidden.shape[0]

    def member(i):
        return (i // 2, place * 2 + lax.rem(i, 2))

    def mate(off):
        return lax.rem(own + off, team)

    def peer(off):
        return lax.rem(place + off, half)

    barrier = pltpu.get_barrier_semaphore()

    def each(count, f):
        def step(off, c):
            f(off)
            return c
        lax.fori_loop(1, count, step, 0)

    def greet(device):
        pl.semaphore_signal(barrier, inc=1, device_id=device, device_id_type=MESH)

    each(team, lambda off: greet(member(mate(off))))
    each(half, lambda off: greet((dp, peer(off) * 2 + core)))
    pl.semaphore_wait(barrier, team + half - 2)

    def remote(src, dst, s, r, device):
        return pltpu.make_async_remote_copy(
            src_ref=src, dst_ref=dst, send_sem=s, recv_sem=r, device_id=device, device_id_type=MESH
        )

    def columns(i):
        return pl.ds(pl.multiple_of(i * width, width), width)

    def copy_gp(off):
        return remote(gp, gps.at[own], sa.at[off], ra.at[off], member(mate(off)))

    def copy_hid(off):
        return remote(
            hidden.at[:, columns(mate(off))], hid.at[own], sb.at[off], rb.at[off], member(mate(off))
        )

    def copy_part(off):
        return remote(
            part.at[peer(off)], got.at[place], sc.at[off], rc.at[off], (dp, peer(off) * 2 + core)
        )

    def copy_sum(off):
        return remote(
            out.at[own, place], out.at[own, place], sd.at[off], rd.at[off],
            (dp, peer(off) * 2 + core),
        )

    def copy_team(off):
        return remote(out.at[own], out.at[own], se.at[off], re.at[off], member(mate(off)))

    each(team, lambda off: copy_gp(off).start())
    each(team, lambda off: copy_hid(off).start())
    gps[own] = gp[...]
    hid[own] = hidden[:, columns(own)]
    each(team, lambda off: copy_gp(off).wait_recv())
    each(team, lambda off: copy_hid(off).wait_recv())
    total = mm(hid[0], gps[0], 0, 0)
    for i in range(1, team):
        total = total + mm(hid[i], gps[i], 0, 0)
    part[...] = total.reshape(part.shape).astype(BF16)
    each(half, lambda off: copy_part(off).start())
    got[place] = part[place]
    each(half, lambda off: copy_part(off).wait_recv())

    def add(i, total):
        return total + got[i].astype(F32)

    out[own, place] = lax.fori_loop(0, half, add, jnp.zeros(got.shape[1:], F32)).astype(BF16)
    each(half, lambda off: copy_sum(off).start())
    each(half, lambda off: copy_sum(off).wait_recv())
    each(half, lambda off: copy_sum(off).wait_send())
    each(team, lambda off: copy_team(off).start())
    each(team, lambda off: copy_team(off).wait_recv())
    each(team, lambda off: copy_team(off).wait_send())
    each(team, lambda off: copy_gp(off).wait_send())
    each(team, lambda off: copy_hid(off).wait_send())
    each(half, lambda off: copy_part(off).wait_send())


def call(kernel, ins, outs, scratch=(), collective=None):
    extra = {} if collective is None else dict(collective_id=collective, has_side_effects=True)
    return pl.pallas_call(
        kernel,
        out_shape=[jax.ShapeDtypeStruct(s, t) for s, t in outs],
        in_specs=[VM] * len(ins),
        out_specs=[VM] * len(outs),
        scratch_shapes=list(scratch),
        compiler_params=pltpu.CompilerParams(vmem_limit_bytes=48 * 2**20, **extra),
    )(*ins)


def scan(state, n, backward):
    slices = state.reshape(n, -1, 128)
    sems = [pltpu.SemaphoreType.DMA((n,))] * 4
    (out,) = call(
        functools.partial(scan_kernel, n, backward), [slices], [(slices.shape, BF16)],
        [pltpu.VMEM(slices.shape, BF16)] * 2 + sems, collective=1 if backward else 0,
    )
    return out.reshape(-1, 128)


def shifted(array, axis, by):
    length = lax.axis_size(axis)
    pairs = [(i, i + by) for i in range(length) if 0 <= i + by < length]
    return lax.ppermute(array, axis, pairs)


def body(n, dps, hidden_in, qk_weight, conv_weight, values, gate_in, cotangent):
    tokens, v, gate, cot = hidden_in[0], values[0], gate_in[0], cotangent[0]
    length, depth = tokens.shape
    cols = qk_weight.shape[1]
    wide = v.shape[1]
    first, second, rows = feature_tables()
    tables = [jnp.asarray(first, BF16), jnp.asarray(second, BF16), jnp.asarray(rows)]
    state_rows = n * 16 * -(-(NORM_ROW + 16) // (16 * n))
    state_shape = ((state_rows, 128), BF16)

    projected = jnp.dot(tokens, qk_weight, preferred_element_type=F32).astype(BF16)
    prev = shifted(projected[length - 8 :], "ctx", 1).astype(F32)
    mixed, own = call(
        key_kernel, [projected, prev, conv_weight, v, *tables], [((length, cols), F32), state_shape]
    )
    before = scan(own, n, False)
    out, ggate, own_grad, dq, dk, dv = call(
        query_kernel,
        [mixed, v, gate, cot, before, *tables],
        [
            ((length, wide), BF16), ((length, wide), BF16), state_shape,
            ((length, cols // 2), F32), ((length, cols // 2), F32), ((length, wide), F32),
        ],
    )
    after = scan(own_grad, n, True)
    gv, gm = call(
        value_kernel, [mixed, v, after, dq, dk, dv, *tables],
        [((length, wide), BF16), ((length, cols), F32)],
    )
    later = shifted(gm[:8], "ctx", -1)
    gp, gh = call(
        hidden_kernel, [gm, later, conv_weight, qk_weight],
        [((length, cols), BF16), ((length, depth), BF16)],
    )
    team, half = 2 * dps, n // 2
    piece = depth // (team * half)
    sem = pltpu.SemaphoreType.DMA
    (gw,) = call(
        functools.partial(weight_kernel, n, dps), [gp, tokens],
        [((team, half, piece, cols), BF16)],
        [
            pltpu.VMEM((team, length, cols), BF16),
            pltpu.VMEM((team, length, depth // team), BF16),
            pltpu.VMEM((half, piece, cols), BF16),
            pltpu.VMEM((half, piece, cols), BF16),
        ]
        + [sem((team,))] * 4 + [sem((half,))] * 4 + [sem((team,))] * 2,
        collective=2,
    )
    return out[None], gh[None], gv[None], ggate[None], gw.reshape(depth, cols)


def solution(mesh):
    split = P("dp", "ctx", None)
    return jax.shard_map(
        functools.partial(body, mesh.shape["ctx"], mesh.shape["dp"]),
        mesh=mesh,
        in_specs=(split, P(), P(), split, split, split),
        out_specs=(split, split, split, split, P()),
        check_vma=False,
    )
```

time: 303 us -> 95.5 us (0.32)
  blocking collectives: 141 us -> 0 us
  Pallas kernels: 0 us -> 83.9 us
  waiting for transfers between devices: 67.5 us -> 2.57 us
  matrix products: 33.7 us -> 1.78 us
  local copies, waits for them, and re-layouts: 28.9 us -> 1.03 us
  between operations: 14.6 us -> 0.8 us
  other arithmetic: 9.88 us -> 0.01 us
    pallas_call x0 -> x7, Pallas kernels: none -> 83.9 us  [call(): pl.pallas_call(kernel, out_shape=[jax.ShapeDtypeStruct(s, t) for s, t in...]
    all_gather x2 -> x0, blocking collectives: 76.1 us -> none  [the longest x1 50.1 us: entering_2(): lax.all_gather(part.astype(kind), axis)]
    all_gather x2 -> x0, waiting for transfers between devices: 67.5 us -> none  [the longest x1 46.4 us: entering(): gathered = jax.tree.map(lambda a: lax.all_gather(a, axis), part)]
    psum x1 -> x0, blocking collectives: 65 us -> none  [body(): grad_qk_weight = lax.psum(local_term, ('dp', 'ctx')).astype(jnp.bfloat16)]
    dot_general x21 -> x1, matrix products: 33.7 us -> 1.78 us  [body(): jnp.dot(tokens, qk_weight, preferred_element_type=F32).astype(BF16)]
    dynamic_slice x32 -> x0, local copies, waits for them, and re-layouts: 19 us -> none  [hop(): part[at].astype(own.dtype)]
    select_n x32 -> x0, other arithmetic: 5.81 us -> none  [hop(): return jax.tree.map(lambda a, b: jnp.where(reached, a, b), new, before)]
    unnamed x53 -> x19, local copies, waits for them, and re-layouts: 5.31 us -> 1.03 us
  transfers between devices with their start and end apart: 4 -> 2, of which waited for: 2 -> 2; matrix products, arithmetic and copies ran while one was open for 7% -> 0% of each run, Pallas kernels for 0% -> 0%
where the time goes in v1:
time: 95.5 us; the launch traced here: 93.8 us
  Pallas kernels  83.9 us (88%)
  starting transfers between devices  3.77 us (4%)
  waiting for transfers between devices  2.57 us (3%)
  matrix products  1.78 us (2%)
  local copies, waits for them, and re-layouts  1.03 us (1%)
    pallas_call x7, Pallas kernels, call(): pl.pallas_call(kernel, out_shape=[jax.ShapeDtypeStruct(s, t) for s, t in...  83.9 us
    ppermute x2, starting transfers between devices, shifted(): return lax.ppermute(array, axis, pairs)  3.77 us
    ppermute x2, waiting for transfers between devices, shifted(): return lax.ppermute(array, axis, pairs)  2.57 us
  transfers between devices with their start and end apart: 2, of which 2 were waited for; matrix products, arithmetic and copies ran while one was open for 0% of the time, Pallas kernels for 0%

profile of v1, /device:TPU:0, one launch (start us, length us, event | category | flops | bytes accessed | tf_op | source)
XLA Modules:
  0.0 93.8 jit_solution(5055197250259277043)
XLA Ops:
  0.6 0.0 copy-start
  0.6 0.0 copy-start.1
  0.7 0.0 copy-start.4
  0.7 0.0 copy-start.5
  0.7 1.8 %convolution_convert_fusion.proj = bf16[128,256]{1,0:T(8,128)(2,1)S(1)} fusion(bf16[2048,256]{1,0:T(8,128)(2,1)} %weight.1, bf16[1,128,2048]{2,1,0:T(8,128)(2,1)} %param.9), kind=kOutput, calls=%fused_computation | convolution fusion | flops 134250496 | bytes 1638400 | tf_op jit(solution)/shard_map/dot_general | solution.py:374
  2.5 0.0 copy-start.8
  2.5 2.4 %collective-permute-start = (bf16[8,256]{1,0:T(8,128)(2,1)S(1)}, bf16[8,256]{1,0:T(8,128)(2,1)S(1)}, u32[]{:S(2)}, u32[]{:S(2)}) collective-permute-start(bf16[8,256]{1,0:T(8,128)(2,1)S(1)} %slice.8), channel_id=1, source_target_pairs={{0,1},{1,2},{2,3},{3,4},{4,5},{5,6},{6,7},{7,8},{8,9},{9,10},{10,1... | collective-permute-start | bytes 12296 | tf_op jit(solution)/shard_map/ppermute | solution.py:361
  4.9 0.8 collective-permute-done
  5.7 0.0 copy-done
  5.7 0.0 copy-done.1
  5.7 0.0 copy-done.4
  5.7 0.0 copy-done.5
  5.7 0.0 copy-done.8
  5.7 1.5 %shard_map.128 = (f32[128,256]{1,0:T(8,128)S(1)}, bf16[768,128]{1,0:T(8,128)(2,1)S(1)}) custom-call(bf16[128,256]{1,0:T(8,128)(2,1)S(1)} %convolution_convert_fusion.proj, f32[8,256]{1,0:T(8,128)S(1)} %convert_element_type.7.prev, f32[3,256]{1,0:T(4,128)S(1)} %copy-done.8, bf16[128,512]{1,0:T(8,128)(2,1)S(1)} %bitcast.18, bf16[128,2048]{1,0:T(8,128)(2,1)S(1)} %copy-done.1, ...), custom_call_target="tpu_custom_call" | custom-call | tf_op jit(solution)/shard_map/pallas_call | solution.py:338
  7.2 0.0 copy-start.6
  7.2 0.0 copy-start.7
  7.2 19.5 %shard_map.129 = bf16[16,48,128]{2,1,0:T(8,128)(2,1)S(1)} custom-call(bf16[16,48,128]{2,1,0:T(8,128)(2,1)S(1)} %bitcast.24), custom_call_target="tpu_custom_call" | custom-call | tf_op jit(solution)/shard_map/pallas_call | solution.py:338
  26.8 0.0 copy-done.6
  26.8 0.0 copy-done.7
  26.8 5.4 %shard_map.130 = (bf16[128,512]{1,0:T(8,128)(2,1)}, bf16[128,512]{1,0:T(8,128)(2,1)}, bf16[768,128]{1,0:T(8,128)(2,1)S(1)}, f32[128,128]{1,0:T(8,128)S(1)}, f32[...) custom-call(f32[128,256]{1,0:T(8,128)S(1)} %get-tuple-element.17.mixed, bf16[128,512]{1,0:T(8,128)(2,1)S(1)} %bitcast.19, ...), custom_call_target="tpu_custom_call" | custom-call | tf_op jit(solution)/shard_map/pallas_call | solution.py:338
  32.2 15.6 %shard_map.131 = bf16[16,48,128]{2,1,0:T(8,128)(2,1)S(1)} custom-call(bf16[16,48,128]{2,1,0:T(8,128)(2,1)S(1)} %bitcast.23), custom_call_target="tpu_custom_call" | custom-call | tf_op jit(solution)/shard_map/pallas_call | solution.py:338
  47.7 0.0 copy-start.2
  47.7 2.5 %shard_map.132 = (bf16[128,512]{1,0:T(8,128)(2,1)}, f32[128,256]{1,0:T(8,128)S(1)}) custom-call(f32[128,256]{1,0:T(8,128)S(1)} %get-tuple-element.17.mixed, bf16[128,512]{1,0:T(8,128)(2,1)S(1)} %bitcast.20, bf16[768,128]{1,0:T(8,128)(2,1)S(1)} %bitcast.22, f32[128,128]{1,0:T(8,128)S(1)} %get-tuple-element.21.dq_in, f32[128,128]{1,0:T(8,128)S(1)} %get-tuple-element.22.dk_in, ...), custom_call_target="tpu_custom_call" | custom-call | tf_op jit(solution)/shard_map/pallas_call | solution.py:338
  50.3 0.0 copy-start.3
  50.3 1.4 %collective-permute-start.1 = (f32[8,256]{1,0:T(8,128)S(1)}, f32[8,256]{1,0:T(8,128)S(1)}, u32[]{:S(2)}, u32[]{:S(2)}) collective-permute-start(f32[8,256]{1,0:T(8,128)S(1)} %slice.7), channel_id=1, source_target_pairs={{1,0},{2,1},{3,2},{4,3},{5,4},{6,5},{7,6},{8,7},{9,8},{10,9},{11,1... | collective-permute-start | bytes 24584 | tf_op jit(solution)/shard_map/ppermute | solution.py:361
  51.7 1.8 %collective-permute-done.1.later = f32[8,256]{1,0:T(8,128)S(1)} collective-permute-done((f32[8,256]{1,0:T(8,128)S(1)}, f32[8,256]{1,0:T(8,128)S(1)}, u32[]{:S(2)}, u32[]{:S(2)}) %collective-permute-start.1) | collective-permute-done | bytes 8224 | tf_op jit(solution)/shard_map/ppermute | solution.py:361
  53.5 0.0 copy-done.2
  53.5 1.3 %shard_map.133 = (bf16[128,256]{1,0:T(8,128)(2,1)S(1)}, bf16[128,2048]{1,0:T(8,128)(2,1)}) custom-call(f32[128,256]{1,0:T(8,128)S(1)} %get-tuple-element.24.gm, f32[8,256]{1,0:T(8,128)S(1)} %collective-permute-done.1.later, f32[3,256]{1,0:T(4,128)S(1)} %copy-done.8, bf16[2048,256]{1,0:T(8,128)(2,1)S(1)} %copy-done.2), custom_call_target="tpu_custom_call" | custom-call | tf_op jit(solution)/shard_map/pallas_call | solution.py:338
  54.7 0.0 copy-done.3
  54.7 38.1 %shard_map.134 = bf16[4,8,64,256]{3,2,1,0:T(8,128)(2,1)S(1)} custom-call(bf16[128,256]{1,0:T(8,128)(2,1)S(1)} %get-tuple-element.28.gp, bf16[128,2048]{1,0:T(8,128)(2,1)S(1)} %bitcast.17), custom_call_target="tpu_custom_call" | custom-call | tf_op jit(solution)/shard_map/pallas_call | solution.py:338
  92.9 1.0 %copy.15 = bf16[2048,256]{1,0:T(8,128)(2,1)} copy(bf16[2048,256]{1,0:T(8,128)(2,1)S(1)} %bitcast.16) | data formatting | bytes 2097152
  (3 shorter events, 0.0 us)
Async XLA Ops:
  0.6 5.0 %copy-start = (bf16[128,2048]{1,0:T(8,128)(2,1)S(1)}, bf16[128,2048]{1,0:T(8,128)(2,1)}, u32[]{:S(2)}) copy-start(bf16[128,2048]{1,0:T(8,128)(2,1)} %constant.7.clone.second) | copy-start | bytes 1572868
  0.6 5.0 %copy-start.1 = (bf16[128,2048]{1,0:T(8,128)(2,1)S(1)}, bf16[128,2048]{1,0:T(8,128)(2,1)}, u32[]{:S(2)}) copy-start(bf16[128,2048]{1,0:T(8,128)(2,1)} %constant.6.clone.first) | copy-start | bytes 1572868
  0.7 5.0 %copy-start.4 = (bf16[1,128,512]{2,1,0:T(8,128)(2,1)S(1)}, bf16[1,128,512]{2,1,0:T(8,128)(2,1)}, u32[]{:S(2)}) copy-start(bf16[1,128,512]{2,1,0:T(8,128)(2,1)} %param.12) | copy-start | bytes 393220
  0.7 5.0 %copy-start.5 = (f32[8,2048]{1,0:T(8,128)S(1)}, f32[8,2048]{1,0:T(8,128)}, u32[]{:S(2)}) copy-start(f32[8,2048]{1,0:T(8,128)} %constant.8.clone.rows) | copy-start | bytes 196612
  2.5 3.2 %copy-start.8 = (f32[3,256]{1,0:T(4,128)S(1)}, f32[3,256]{1,0:T(4,128)}, u32[]{:S(2)}) copy-start(f32[3,256]{1,0:T(4,128)} %conv.3) | copy-start | bytes 9220
  2.5 3.2 %collective-permute-start = (bf16[8,256]{1,0:T(8,128)(2,1)S(1)}, bf16[8,256]{1,0:T(8,128)(2,1)S(1)}, u32[]{:S(2)}, u32[]{:S(2)}) collective-permute-start(bf16[8,256]{1,0:T(8,128)(2,1)S(1)} %slice.8), channel_id=1, source_target_pairs={{0,1},{1,2},{2,3},{3,4},{4,5},{5,6},{6,7},{7,8},{8,9},{9,10},{10,1... | collective-permute-start | bytes 12296 | tf_op jit(solution)/shard_map/ppermute | solution.py:361
  7.2 19.6 %copy-start.6 = (bf16[1,128,512]{2,1,0:T(8,128)(2,1)S(1)}, bf16[1,128,512]{2,1,0:T(8,128)(2,1)}, u32[]{:S(2)}) copy-start(bf16[1,128,512]{2,1,0:T(8,128)(2,1)} %param.13) | copy-start | bytes 393220
  7.2 19.6 %copy-start.7 = (bf16[1,128,512]{2,1,0:T(8,128)(2,1)S(1)}, bf16[1,128,512]{2,1,0:T(8,128)(2,1)}, u32[]{:S(2)}) copy-start(bf16[1,128,512]{2,1,0:T(8,128)(2,1)} %param.14) | copy-start | bytes 393220
  47.7 5.7 %copy-start.2 = (bf16[2048,256]{1,0:T(8,128)(2,1)S(1)}, bf16[2048,256]{1,0:T(8,128)(2,1)}, u32[]{:S(2)}) copy-start(bf16[2048,256]{1,0:T(8,128)(2,1)} %weight.1) | copy-start | bytes 3145732
  50.3 4.5 %copy-start.3 = (bf16[1,128,2048]{2,1,0:T(8,128)(2,1)S(1)}, bf16[1,128,2048]{2,1,0:T(8,128)(2,1)}, u32[]{:S(2)}) copy-start(bf16[1,128,2048]{2,1,0:T(8,128)(2,1)} %param.9) | copy-start | bytes 1572868
  50.3 3.2 %collective-permute-start.1 = (f32[8,256]{1,0:T(8,128)S(1)}, f32[8,256]{1,0:T(8,128)S(1)}, u32[]{:S(2)}, u32[]{:S(2)}) collective-permute-start(f32[8,256]{1,0:T(8,128)S(1)} %slice.7), channel_id=1, source_target_pairs={{1,0},{2,1},{3,2},{4,3},{5,4},{6,5},{7,6},{8,7},{9,8},{10,9},{11,1... | collective-permute-start | bytes 24584 | tf_op jit(solution)/shard_map/ppermute | solution.py:361

commit v2 on v1

--- a/solution.py
+++ b/solution.py
@@ -190,9 +190,18 @@
     gh[...] = mm(gp, weight[...], 1, 1).astype(BF16)
 
 
-def scan_kernel(n, backward, state, out, got, sums, send1, recv1, send2, recv2):
+def scan_kernel(n, dps, backward, *refs):
+    if backward:
+        state, out, got, sums, send1, recv1, send2, recv2 = refs
+        team = 1
+    else:
+        state, hidden, out, hid, got, sums, send1, recv1, send2, recv2, send3, recv3 = refs
+        team = 2 * dps
+        width = hidden.shape[1] // team
     me = lax.axis_index("ctx")
     dp = lax.axis_index("dp")
+    core, place = lax.rem(me, 2), me // 2
+    mine = dp * 2 + core
 
     def peer(off):
         return lax.rem(me + off, n)
@@ -203,8 +212,25 @@
         pl.semaphore_signal(barrier, inc=1, device_id=(dp, peer(off)), device_id_type=MESH)
         return c
 
+    def mate(off):
+        return lax.rem(mine + off, team)
+
+    def member(i):
+        return (i // 2, place * 2 + lax.rem(i, 2))
+
+    def columns(i):
+        return pl.ds(pl.multiple_of(i * width, width), width)
+
+    def copy3(off):
+        return pltpu.make_async_remote_copy(
+            src_ref=hidden.at[:, columns(mate(off))], dst_ref=hid.at[mine], send_sem=send3.at[off],
+            recv_sem=recv3.at[off], device_id=member(mate(off)), device_id_type=MESH,
+        )
+
     lax.fori_loop(1, n, greet, 0)
-    pl.semaphore_wait(barrier, n - 1)
+    for off in range(1, team):
+        pl.semaphore_signal(barrier, inc=1, device_id=member(mate(off)), device_id_type=MESH)
+    pl.semaphore_wait(barrier, n + team - 2)
 
     def copy1(off):
         return pltpu.make_async_remote_copy(
@@ -225,6 +251,10 @@
         lax.fori_loop(1, n, step, 0)
 
     each(lambda off: copy1(off).start())
+    for off in range(1, team):
+        copy3(off).start()
+    if team > 1:
+        hid[mine] = hidden[:, columns(mine)]
     got[me] = state[me]
     each(lambda off: copy1(off).wait_recv())
 
@@ -239,16 +269,16 @@
     each(lambda off: copy2(off).wait_recv())
     each(lambda off: copy1(off).wait_send())
     each(lambda off: copy2(off).wait_send())
-
-
-def weight_kernel(n, dps, gp, hidden, out, gps, hid, part, got, sa, ra, sb, rb, sc, rc, sd, rd, se, re):
+    for off in range(1, team):
+        copy3(off).wait()
+
+
+def weight_kernel(n, dps, gp, hid, out, gps, part, got, sa, ra, sc, rc, sd, rd, sx, rx, sy, ry):
     dp, me = lax.axis_index("dp"), lax.axis_index("ctx")
     half = n // 2
     core, place = lax.rem(me, 2), me // 2
     own = dp * 2 + core
     team = dps * 2
-    width = hidden.shape[1] // team
-    tokens = hidden.shape[0]
 
     def member(i):
         return (i // 2, place * 2 + lax.rem(i, 2))
@@ -259,13 +289,19 @@
     def peer(off):
         return lax.rem(place + off, half)
 
+    def side(off):
+        return lax.rem(dp + off, dps)
+
+    def slot(off):
+        return lax.rem(place + half - off, half)
+
     barrier = pltpu.get_barrier_semaphore()
 
-    def each(count, f):
+    def each(count, f, least=1):
         def step(off, c):
             f(off)
             return c
-        lax.fori_loop(1, count, step, 0)
+        lax.fori_loop(least, count, step, 0)
 
     def greet(device):
         pl.semaphore_signal(barrier, inc=1, device_id=device, device_id_type=MESH)
@@ -279,16 +315,8 @@
             src_ref=src, dst_ref=dst, send_sem=s, recv_sem=r, device_id=device, device_id_type=MESH
         )
 
-    def columns(i):
-        return pl.ds(pl.multiple_of(i * width, width), width)
-
     def copy_gp(off):
         return remote(gp, gps.at[own], sa.at[off], ra.at[off], member(mate(off)))
-
-    def copy_hid(off):
-        return remote(
-            hidden.at[:, columns(mate(off))], hid.at[own], sb.at[off], rb.at[off], member(mate(off))
-        )
 
     def copy_part(off):
         return remote(
@@ -301,15 +329,17 @@
             (dp, peer(off) * 2 + core),
         )
 
-    def copy_team(off):
-        return remote(out.at[own], out.at[own], se.at[off], re.at[off], member(mate(off)))
+    def copy_side(d, off):
+        ref = out.at[own, slot(off)]
+        return remote(ref, ref, sx.at[d, off], rx.at[d, off], (side(d), me))
+
+    def copy_core(d, off):
+        ref = out.at[side(d) * 2 + core, slot(off)]
+        return remote(ref, ref, sy.at[d, off], ry.at[d, off], (dp, place * 2 + 1 - core))
 
     each(team, lambda off: copy_gp(off).start())
-    each(team, lambda off: copy_hid(off).start())
     gps[own] = gp[...]
-    hid[own] = hidden[:, columns(own)]
     each(team, lambda off: copy_gp(off).wait_recv())
-    each(team, lambda off: copy_hid(off).wait_recv())
     total = mm(hid[0], gps[0], 0, 0)
     for i in range(1, team):
         total = total + mm(hid[i], gps[i], 0, 0)
@@ -323,13 +353,41 @@
 
     out[own, place] = lax.fori_loop(0, half, add, jnp.zeros(got.shape[1:], F32)).astype(BF16)
     each(half, lambda off: copy_sum(off).start())
-    each(half, lambda off: copy_sum(off).wait_recv())
+
+    def hand_on(off):
+        for d in range(1, dps):
+            copy_side(d, off).start()
+        copy_core(0, off).start()
+
+    def take_side(off):
+        for d in range(1, dps):
+            copy_side(d, off).wait_recv()
+            copy_core(d, off).start()
+
+    hand_on(0)
+
+    def arrive(off):
+        copy_sum(off).wait_recv()
+        hand_on(off)
+        take_side(off - 1)
+
+    each(half, arrive)
+    take_side(half - 1)
+
+    def finish(off):
+        for d in range(dps):
+            copy_core(d, off).wait_recv()
+
+    def sent(off):
+        for d in range(dps):
+            copy_core(d, off).wait_send()
+        for d in range(1, dps):
+            copy_side(d, off).wait_send()
+
+    each(half, finish, 0)
+    each(half, sent, 0)
     each(half, lambda off: copy_sum(off).wait_send())
-    each(team, lambda off: copy_team(off).start())
-    each(team, lambda off: copy_team(off).wait_recv())
-    each(team, lambda off: copy_team(off).wait_send())
     each(team, lambda off: copy_gp(off).wait_send())
-    each(team, lambda off: copy_hid(off).wait_send())
     each(half, lambda off: copy_part(off).wait_send())
 
 
@@ -345,14 +403,20 @@
     )(*ins)
 
 
-def scan(state, n, backward):
+def scan(state, n, dps, hidden=None):
     slices = state.reshape(n, -1, 128)
+    ins, outs = [slices], [(slices.shape, BF16)]
     sems = [pltpu.SemaphoreType.DMA((n,))] * 4
-    (out,) = call(
-        functools.partial(scan_kernel, n, backward), [slices], [(slices.shape, BF16)],
-        [pltpu.VMEM(slices.shape, BF16)] * 2 + sems, collective=1 if backward else 0,
-    )
-    return out.reshape(-1, 128)
+    if hidden is not None:
+        team = 2 * dps
+        ins.append(hidden)
+        outs.append(((team, hidden.shape[0], hidden.shape[1] // team), BF16))
+        sems = sems + [pltpu.SemaphoreType.DMA((team,))] * 2
+    out, *rest = call(
+        functools.partial(scan_kernel, n, dps, hidden is None), ins, outs,
+        [pltpu.VMEM(slices.shape, BF16)] * 2 + sems, collective=1 if hidden is None else 0,
+    )
+    return out.reshape(-1, 128), *rest
 
 
 def shifted(array, axis, by):
@@ -376,7 +440,7 @@
     mixed, own = call(
         key_kernel, [projected, prev, conv_weight, v, *tables], [((length, cols), F32), state_shape]
     )
-    before = scan(own, n, False)
+    before, hid = scan(own, n, dps, tokens)
     out, ggate, own_grad, dq, dk, dv = call(
         query_kernel,
         [mixed, v, gate, cot, before, *tables],
@@ -385,7 +449,7 @@
             ((length, cols // 2), F32), ((length, cols // 2), F32), ((length, wide), F32),
         ],
     )
-    after = scan(own_grad, n, True)
+    (after,) = scan(own_grad, n, dps)
     gv, gm = call(
         value_kernel, [mixed, v, after, dq, dk, dv, *tables],
         [((length, wide), BF16), ((length, cols), F32)],
@@ -399,15 +463,14 @@
     piece = depth // (team * half)
     sem = pltpu.SemaphoreType.DMA
     (gw,) = call(
-        functools.partial(weight_kernel, n, dps), [gp, tokens],
+        functools.partial(weight_kernel, n, dps), [gp, hid],
         [((team, half, piece, cols), BF16)],
         [
             pltpu.VMEM((team, length, cols), BF16),
-            pltpu.VMEM((team, length, depth // team), BF16),
             pltpu.VMEM((half, piece, cols), BF16),
             pltpu.VMEM((half, piece, cols), BF16),
         ]
-        + [sem((team,))] * 4 + [sem((half,))] * 4 + [sem((team,))] * 2,
+        + [sem((team,))] * 2 + [sem((half,))] * 4 + [sem((dps, half))] * 4,
         collective=2,
     )
     return out[None], gh[None], gv[None], ggate[None], gw.reshape(depth, cols)

time: 95.5 us -> 92.5 us (0.969); the launches traced: 93.8 us -> 92.3 us
  Pallas kernels: 83.9 us -> 82.5 us
    pallas_call x7, Pallas kernels: 83.9 us -> 82.5 us  [call(): pl.pallas_call(kernel, out_shape=[jax.ShapeDtypeStruct(s, t) for s, t in...]
where the time goes in v2:
time: 92.5 us; the launch traced here: 92.3 us
  Pallas kernels  82.5 us (89%)
  starting transfers between devices  3.64 us (4%)
  waiting for transfers between devices  2.57 us (3%)
  matrix products  1.78 us (2%)
  local copies, waits for them, and re-layouts  1.03 us (1%)
    pallas_call x7, Pallas kernels, call(): pl.pallas_call(kernel, out_shape=[jax.ShapeDtypeStruct(s, t) for s, t in...  82.5 us
    ppermute x2, starting transfers between devices, shifted(): return lax.ppermute(array, axis, pairs)  3.64 us
    ppermute x2, waiting for transfers between devices, shifted(): return lax.ppermute(array, axis, pairs)  2.57 us
  transfers between devices with their start and end apart: 2, of which 2 were waited for; matrix products, arithmetic and copies ran while one was open for 0% of the time, Pallas kernels for 0%

profile of v2, /device:TPU:0, one launch (start us, length us, event | category | flops | bytes accessed | tf_op | source)
XLA Modules:
  0.0 92.3 jit_solution(7847328063906016062)
XLA Ops:
  0.6 0.0 copy-start
  0.6 0.0 copy-start.1
  0.7 0.0 copy-start.4
  0.7 0.0 copy-start.5
  0.7 1.8 %convolution_convert_fusion.proj = bf16[128,256]{1,0:T(8,128)(2,1)S(1)} fusion(bf16[2048,256]{1,0:T(8,128)(2,1)} %weight.1, bf16[1,128,2048]{2,1,0:T(8,128)(2,1)} %param.9), kind=kOutput, calls=%fused_computation | convolution fusion | flops 134250496 | bytes 1638400 | tf_op jit(solution)/shard_map/dot_general | solution.py:438
  2.5 0.0 copy-start.8
  2.5 2.4 %collective-permute-start = (bf16[8,256]{1,0:T(8,128)(2,1)S(1)}, bf16[8,256]{1,0:T(8,128)(2,1)S(1)}, u32[]{:S(2)}, u32[]{:S(2)}) collective-permute-start(bf16[8,256]{1,0:T(8,128)(2,1)S(1)} %slice.8), channel_id=1, source_target_pairs={{0,1},{1,2},{2,3},{3,4},{4,5},{5,6},{6,7},{7,8},{8,9},{9,10},{10,1... | collective-permute-start | bytes 12296 | tf_op jit(solution)/shard_map/ppermute | solution.py:425
  4.9 0.8 collective-permute-done
  5.7 0.0 copy-done
  5.7 0.0 copy-done.1
  5.7 0.0 copy-done.4
  5.7 0.0 copy-done.5
  5.7 0.0 copy-done.8
  5.7 0.0 copy-start.3
  5.7 1.5 %shard_map.128 = (f32[128,256]{1,0:T(8,128)S(1)}, bf16[768,128]{1,0:T(8,128)(2,1)S(1)}) custom-call(bf16[128,256]{1,0:T(8,128)(2,1)S(1)} %convolution_convert_fusion.proj, f32[8,256]{1,0:T(8,128)S(1)} %convert_element_type.7.prev, f32[3,256]{1,0:T(4,128)S(1)} %copy-done.8, bf16[128,512]{1,0:T(8,128)(2,1)S(1)} %bitcast.18, bf16[128,2048]{1,0:T(8,128)(2,1)S(1)} %copy-done.1, ...), custom_call_target="tpu_custom_call" | custom-call | tf_op jit(solution)/shard_map/pallas_call | solution.py:396
  7.2 0.0 copy-done.3
  7.2 0.0 copy-start.6
  7.2 0.0 copy-start.7
  7.3 19.6 %shard_map.129 = (bf16[16,48,128]{2,1,0:T(8,128)(2,1)S(1)}, bf16[4,128,512]{2,1,0:T(8,128)(2,1)S(1)}) custom-call(bf16[16,48,128]{2,1,0:T(8,128)(2,1)S(1)} %bitcast.24, bf16[128,2048]{1,0:T(8,128)(2,1)S(1)} %bitcast.17), custom_call_target="tpu_custom_call" | custom-call | tf_op jit(solution)/shard_map/pallas_call | solution.py:396
  26.9 0.0 copy-done.6
  26.9 0.0 copy-done.7
  26.9 5.4 %shard_map.130 = (bf16[128,512]{1,0:T(8,128)(2,1)}, bf16[128,512]{1,0:T(8,128)(2,1)}, bf16[768,128]{1,0:T(8,128)(2,1)S(1)}, f32[128,128]{1,0:T(8,128)S(1)}, f32[...) custom-call(f32[128,256]{1,0:T(8,128)S(1)} %get-tuple-element.19.mixed, bf16[128,512]{1,0:T(8,128)(2,1)S(1)} %bitcast.19, ...), custom_call_target="tpu_custom_call" | custom-call | tf_op jit(solution)/shard_map/pallas_call | solution.py:396
  32.3 15.9 %shard_map.131 = bf16[16,48,128]{2,1,0:T(8,128)(2,1)S(1)} custom-call(bf16[16,48,128]{2,1,0:T(8,128)(2,1)S(1)} %bitcast.23), custom_call_target="tpu_custom_call" | custom-call | tf_op jit(solution)/shard_map/pallas_call | solution.py:396
  48.2 0.0 copy-start.2
  48.2 2.5 %shard_map.132 = (bf16[128,512]{1,0:T(8,128)(2,1)}, f32[128,256]{1,0:T(8,128)S(1)}) custom-call(f32[128,256]{1,0:T(8,128)S(1)} %get-tuple-element.19.mixed, bf16[128,512]{1,0:T(8,128)(2,1)S(1)} %bitcast.20, bf16[768,128]{1,0:T(8,128)(2,1)S(1)} %bitcast.21, f32[128,128]{1,0:T(8,128)S(1)} %get-tuple-element.24.dq_in, f32[128,128]{1,0:T(8,128)S(1)} %get-tuple-element.25.dk_in, ...), custom_call_target="tpu_custom_call" | custom-call | tf_op jit(solution)/shard_map/pallas_call | solution.py:396
  50.8 1.3 %collective-permute-start.1 = (f32[8,256]{1,0:T(8,128)S(1)}, f32[8,256]{1,0:T(8,128)S(1)}, u32[]{:S(2)}, u32[]{:S(2)}) collective-permute-start(f32[8,256]{1,0:T(8,128)S(1)} %slice.7), channel_id=1, source_target_pairs={{1,0},{2,1},{3,2},{4,3},{5,4},{6,5},{7,6},{8,7},{9,8},{10,9},{11,1... | collective-permute-start | bytes 24584 | tf_op jit(solution)/shard_map/ppermute | solution.py:425
  52.0 1.8 %collective-permute-done.1.later = f32[8,256]{1,0:T(8,128)S(1)} collective-permute-done((f32[8,256]{1,0:T(8,128)S(1)}, f32[8,256]{1,0:T(8,128)S(1)}, u32[]{:S(2)}, u32[]{:S(2)}) %collective-permute-start.1) | collective-permute-done | bytes 8224 | tf_op jit(solution)/shard_map/ppermute | solution.py:425
  53.8 0.0 copy-done.2
  53.8 1.3 %shard_map.133 = (bf16[128,256]{1,0:T(8,128)(2,1)S(1)}, bf16[128,2048]{1,0:T(8,128)(2,1)}) custom-call(f32[128,256]{1,0:T(8,128)S(1)} %get-tuple-element.27.gm, f32[8,256]{1,0:T(8,128)S(1)} %collective-permute-done.1.later, f32[3,256]{1,0:T(4,128)S(1)} %copy-done.8, bf16[2048,256]{1,0:T(8,128)(2,1)S(1)} %copy-done.2), custom_call_target="tpu_custom_call" | custom-call | tf_op jit(solution)/shard_map/pallas_call | solution.py:396
  55.1 36.2 %shard_map.134 = bf16[4,8,64,256]{3,2,1,0:T(8,128)(2,1)S(1)} custom-call(bf16[128,256]{1,0:T(8,128)(2,1)S(1)} %get-tuple-element.31.gp, bf16[4,128,512]{2,1,0:T(8,128)(2,1)S(1)} %get-tuple-element.32.hid), custom_call_target="tpu_custom_call" | custom-call | tf_op jit(solution)/shard_map/pallas_call | solution.py:396
  91.3 1.0 %copy.15 = bf16[2048,256]{1,0:T(8,128)(2,1)} copy(bf16[2048,256]{1,0:T(8,128)(2,1)S(1)} %bitcast.16) | data formatting | bytes 2097152
  (3 shorter events, 0.0 us)
Async XLA Ops:
  0.6 5.0 %copy-start = (bf16[128,2048]{1,0:T(8,128)(2,1)S(1)}, bf16[128,2048]{1,0:T(8,128)(2,1)}, u32[]{:S(2)}) copy-start(bf16[128,2048]{1,0:T(8,128)(2,1)} %constant.7.clone.second) | copy-start | bytes 1572868
  0.6 5.0 %copy-start.1 = (bf16[128,2048]{1,0:T(8,128)(2,1)S(1)}, bf16[128,2048]{1,0:T(8,128)(2,1)}, u32[]{:S(2)}) copy-start(bf16[128,2048]{1,0:T(8,128)(2,1)} %constant.6.clone.first) | copy-start | bytes 1572868
  0.7 5.0 %copy-start.4 = (bf16[1,128,512]{2,1,0:T(8,128)(2,1)S(1)}, bf16[1,128,512]{2,1,0:T(8,128)(2,1)}, u32[]{:S(2)}) copy-start(bf16[1,128,512]{2,1,0:T(8,128)(2,1)} %param.12) | copy-start | bytes 393220
  0.7 5.0 %copy-start.5 = (f32[8,2048]{1,0:T(8,128)S(1)}, f32[8,2048]{1,0:T(8,128)}, u32[]{:S(2)}) copy-start(f32[8,2048]{1,0:T(8,128)} %constant.8.clone.rows) | copy-start | bytes 196612
  2.5 3.2 %copy-start.8 = (f32[3,256]{1,0:T(4,128)S(1)}, f32[3,256]{1,0:T(4,128)}, u32[]{:S(2)}) copy-start(f32[3,256]{1,0:T(4,128)} %conv.3) | copy-start | bytes 9220
  2.5 3.2 %collective-permute-start = (bf16[8,256]{1,0:T(8,128)(2,1)S(1)}, bf16[8,256]{1,0:T(8,128)(2,1)S(1)}, u32[]{:S(2)}, u32[]{:S(2)}) collective-permute-start(bf16[8,256]{1,0:T(8,128)(2,1)S(1)} %slice.8), channel_id=1, source_target_pairs={{0,1},{1,2},{2,3},{3,4},{4,5},{5,6},{6,7},{7,8},{8,9},{9,10},{10,1... | collective-permute-start | bytes 12296 | tf_op jit(solution)/shard_map/ppermute | solution.py:425
  5.7 1.5 %copy-start.3 = (bf16[1,128,2048]{2,1,0:T(8,128)(2,1)S(1)}, bf16[1,128,2048]{2,1,0:T(8,128)(2,1)}, u32[]{:S(2)}) copy-start(bf16[1,128,2048]{2,1,0:T(8,128)(2,1)} %param.9) | copy-start | bytes 1572868
  7.2 19.7 %copy-start.6 = (bf16[1,128,512]{2,1,0:T(8,128)(2,1)S(1)}, bf16[1,128,512]{2,1,0:T(8,128)(2,1)}, u32[]{:S(2)}) copy-start(bf16[1,128,512]{2,1,0:T(8,128)(2,1)} %param.13) | copy-start | bytes 393220
  7.2 19.7 %copy-start.7 = (bf16[1,128,512]{2,1,0:T(8,128)(2,1)S(1)}, bf16[1,128,512]{2,1,0:T(8,128)(2,1)}, u32[]{:S(2)}) copy-start(bf16[1,128,512]{2,1,0:T(8,128)(2,1)} %param.14) | copy-start | bytes 393220
  48.2 5.6 %copy-start.2 = (bf16[2048,256]{1,0:T(8,128)(2,1)S(1)}, bf16[2048,256]{1,0:T(8,128)(2,1)}, u32[]{:S(2)}) copy-start(bf16[2048,256]{1,0:T(8,128)(2,1)} %weight.1) | copy-start | bytes 3145732
  50.8 3.1 %collective-permute-start.1 = (f32[8,256]{1,0:T(8,128)S(1)}, f32[8,256]{1,0:T(8,128)S(1)}, u32[]{:S(2)}, u32[]{:S(2)}) collective-permute-start(f32[8,256]{1,0:T(8,128)S(1)} %slice.7), channel_id=1, source_target_pairs={{1,0},{2,1},{3,2},{4,3},{5,4},{6,5},{7,6},{8,7},{9,8},{10,9},{11,1... | collective-permute-start | bytes 24584 | tf_op jit(solution)/shard_map/ppermute | solution.py:425

commit v3 on v1

--- a/solution.py
+++ b/solution.py
@@ -190,147 +190,236 @@
     gh[...] = mm(gp, weight[...], 1, 1).astype(BF16)
 
 
-def scan_kernel(n, backward, state, out, got, sums, send1, recv1, send2, recv2):
-    me = lax.axis_index("ctx")
-    dp = lax.axis_index("dp")
+def remote(src, dst, s, r, device):
+    return pltpu.make_async_remote_copy(
+        src_ref=src, dst_ref=dst, send_sem=s, recv_sem=r, device_id=device, device_id_type=MESH
+    )
+
+
+def each(count, f, least=1):
+    if count <= least:
+        return
+
+    def step(off, c):
+        f(off)
+        return c
+
+    lax.fori_loop(least, count, step, 0)
+
+
+def greet(device):
+    pl.semaphore_signal(
+        pltpu.get_barrier_semaphore(), inc=1, device_id=device, device_id_type=MESH
+    )
+
+
+def scan_kernel(n, backward, *refs):
+    if backward:
+        state, out, theirs, both, got, sums, give, *sems = refs
+        team = 1
+    else:
+        state, hidden, out, hid, theirs, both, got, sums, give, *sems = refs
+        team = 8
+        width = hidden.shape[1] // team
+        sh, rh = sems[8:]
+    s0, r0, s1, r1, s2, r2, s3, r3 = sems[:8]
+    dp, me = lax.axis_index("dp"), lax.axis_index("ctx")
+    core, pair = lax.rem(me, 2), me // 2
+    half = n // 2
+    other = (dp, pair * 2 + 1 - core)
+    mine = dp * 4 + lax.rem(me, 4)
 
     def peer(off):
-        return lax.rem(me + off, n)
+        return lax.rem(pair + off, half)
+
+    def slot(off):
+        return lax.rem(pair + half - off, half)
+
+    def far(off):
+        return (dp, peer(off) * 2 + core)
+
+    def mate(off):
+        return lax.rem(mine + off, team)
+
+    def member(i):
+        return (i // 4, me // 4 * 4 + lax.rem(i, 4))
+
+    def columns(i):
+        return pl.ds(pl.multiple_of(i * width, width), width)
+
+    def copy0():
+        return remote(state.at[1 - core], theirs, s0.at[0], r0.at[0], other)
+
+    def copy1(off):
+        return remote(both.at[peer(off)], got.at[pair], s1.at[off], r1.at[off], far(off))
+
+    def copy2(off):
+        return remote(sums.at[peer(off)], give.at[0, pair], s2.at[off], r2.at[off], far(off))
+
+    def copy3(off):
+        at = slot(off)
+        return remote(give.at[1, at], out.at[core, at], s3.at[off], r3.at[off], other)
+
+    def copy_hid(off):
+        return remote(
+            hidden.at[:, columns(mate(off))], hid.at[mine], sh.at[off], rh.at[off], member(mate(off))
+        )
 
     barrier = pltpu.get_barrier_semaphore()
-
-    def greet(off, c):
-        pl.semaphore_signal(barrier, inc=1, device_id=(dp, peer(off)), device_id_type=MESH)
-        return c
-
-    lax.fori_loop(1, n, greet, 0)
-    pl.semaphore_wait(barrier, n - 1)
-
-    def copy1(off):
-        return pltpu.make_async_remote_copy(
-            src_ref=state.at[peer(off)], dst_ref=got.at[me], send_sem=send1.at[off],
-            recv_sem=recv1.at[off], device_id=(dp, peer(off)), device_id_type=MESH,
-        )
-
-    def copy2(off):
-        return pltpu.make_async_remote_copy(
-            src_ref=sums.at[peer(off)], dst_ref=out.at[me], send_sem=send2.at[off],
-            recv_sem=recv2.at[off], device_id=(dp, peer(off)), device_id_type=MESH,
-        )
-
-    def each(f):
-        def step(off, c):
-            f(off)
-            return c
-        lax.fori_loop(1, n, step, 0)
-
-    each(lambda off: copy1(off).start())
-    got[me] = state[me]
-    each(lambda off: copy1(off).wait_recv())
+    greet(other)
+    each(half, lambda off: greet(far(off)))
+    each(team, lambda off: greet(member(mate(off))))
+    pl.semaphore_wait(barrier, half + team - 1)
+
+    copy0().start()
+    each(team, lambda off: copy_hid(off).start())
+    if team > 1:
+        hid[mine] = hidden[:, columns(mine)]
+    copy0().wait_recv()
+    both[...] = (state[core].astype(F32) + theirs[...].astype(F32)).astype(BF16)
+    each(half, lambda off: copy1(off).start())
+    got[pair] = both[pair]
+    each(half, lambda off: copy1(off).wait_recv())
 
     def add(i, total):
-        at = n - 1 - i if backward else i
+        at = half - 1 - i if backward else i
         sums[at] = total.astype(BF16)
         return total + got[at].astype(F32)
 
-    lax.fori_loop(0, n, add, jnp.zeros(got.shape[1:], F32))
-    each(lambda off: copy2(off).start())
-    out[me] = sums[me]
-    each(lambda off: copy2(off).wait_recv())
-    each(lambda off: copy1(off).wait_send())
-    each(lambda off: copy2(off).wait_send())
-
-
-def weight_kernel(n, dps, gp, hidden, out, gps, hid, part, got, sa, ra, sb, rb, sc, rc, sd, rd, se, re):
+    lax.fori_loop(0, half, add, jnp.zeros(got.shape[1:], F32))
+    each(half, lambda off: copy2(off).start())
+    give[0, pair] = sums[pair]
+    late = core if not backward else 1 - core
+    mine_late = late.astype(F32)
+    other_late = 1.0 - mine_late
+
+    def hand_on(off):
+        at = slot(off)
+        before = give[0, at].astype(F32)
+        out[core, at] = (before + mine_late * theirs[at].astype(F32)).astype(BF16)
+        give[1, at] = (before + other_late * state[core, at].astype(F32)).astype(BF16)
+        copy3(off).start()
+
+    def arrive(off):
+        copy2(off).wait_recv()
+        hand_on(off)
+
+    hand_on(0)
+    each(half, arrive)
+    each(half, lambda off: copy3(off).wait_recv(), 0)
+    each(half, lambda off: copy3(off).wait_send(), 0)
+    each(half, lambda off: copy2(off).wait_send())
+    each(half, lambda off: copy1(off).wait_send())
+    copy0().wait_send()
+    each(team, lambda off: copy_hid(off).wait())
+
+
+def weight_kernel(n, gp, hid, out, gps, part, got, sa, ra, sb, rb, sc, rc, sd, rd, se, re):
     dp, me = lax.axis_index("dp"), lax.axis_index("ctx")
-    half = n // 2
-    core, place = lax.rem(me, 2), me // 2
-    own = dp * 2 + core
-    team = dps * 2
-    width = hidden.shape[1] // team
-    tokens = hidden.shape[0]
-
-    def member(i):
-        return (i // 2, place * 2 + lax.rem(i, 2))
-
-    def mate(off):
-        return lax.rem(own + off, team)
+    count = n // 4
+    place, sub = me // 4, lax.rem(me, 4)
+    row, core = sub // 2, lax.rem(sub, 2)
+    own = dp * 4 + sub
 
     def peer(off):
-        return lax.rem(place + off, half)
+        return lax.rem(place + off, count)
+
+    def slot(off):
+        return lax.rem(place + count - off, count)
+
+    def far(off):
+        return (dp, peer(off) * 4 + sub)
+
+    def side(dx, dy):
+        return lax.rem(dp + dx, 2), lax.rem(row + dy, 2) * 2 + core
+
+    def device(dx, dy):
+        x, low = side(dx, dy)
+        return (x, place * 4 + low)
+
+    def ident(dx, dy):
+        x, low = side(dx, dy)
+        return x * 4 + low
+
+    other = (dp, place * 4 + row * 2 + 1 - core)
+    sides = [(0, 0), (0, 1), (1, 0), (1, 1)]
+
+    def copy_gp(r):
+        return remote(gp, gps.at[own], sa.at[r], ra.at[r], device(*sides[r]))
+
+    def copy_gp_on(r):
+        ref = gps.at[ident(*sides[r])]
+        return remote(gp if r == 0 else ref, ref, sb.at[r], rb.at[r], other)
+
+    def copy_part(off):
+        return remote(part.at[peer(off)], got.at[place], sc.at[off], rc.at[off], far(off))
+
+    def copy_sum(off):
+        ref = out.at[own, place]
+        return remote(ref, ref, sd.at[off], rd.at[off], far(off))
+
+    def copy_on(key, off):
+        first, second = ((0, 1), (1, 0)) if off % 2 == 0 else ((1, 0), (0, 1))
+        source = ((0, 0), (0, 0), first, (0, 0), first, second, (1, 1))[key]
+        target = other if key > 2 else device(*(first if key == 0 else second))
+        ref = out.at[ident(*source), slot(off)]
+        return remote(ref, ref, se.at[key, off], re.at[key, off], target)
 
     barrier = pltpu.get_barrier_semaphore()
-
-    def each(count, f):
-        def step(off, c):
-            f(off)
-            return c
-        lax.fori_loop(1, count, step, 0)
-
-    def greet(device):
-        pl.semaphore_signal(barrier, inc=1, device_id=device, device_id_type=MESH)
-
-    each(team, lambda off: greet(member(mate(off))))
-    each(half, lambda off: greet((dp, peer(off) * 2 + core)))
-    pl.semaphore_wait(barrier, team + half - 2)
-
-    def remote(src, dst, s, r, device):
-        return pltpu.make_async_remote_copy(
-            src_ref=src, dst_ref=dst, send_sem=s, recv_sem=r, device_id=device, device_id_type=MESH
-        )
-
-    def columns(i):
-        return pl.ds(pl.multiple_of(i * width, width), width)
-
-    def copy_gp(off):
-        return remote(gp, gps.at[own], sa.at[off], ra.at[off], member(mate(off)))
-
-    def copy_hid(off):
-        return remote(
-            hidden.at[:, columns(mate(off))], hid.at[own], sb.at[off], rb.at[off], member(mate(off))
-        )
-
-    def copy_part(off):
-        return remote(
-            part.at[peer(off)], got.at[place], sc.at[off], rc.at[off], (dp, peer(off) * 2 + core)
-        )
-
-    def copy_sum(off):
-        return remote(
-            out.at[own, place], out.at[own, place], sd.at[off], rd.at[off],
-            (dp, peer(off) * 2 + core),
-        )
-
-    def copy_team(off):
-        return remote(out.at[own], out.at[own], se.at[off], re.at[off], member(mate(off)))
-
-    each(team, lambda off: copy_gp(off).start())
-    each(team, lambda off: copy_hid(off).start())
+    greet(other)
+    for r in range(1, 4):
+        greet(device(*sides[r]))
+    each(count, lambda off: greet(far(off)))
+    pl.semaphore_wait(barrier, count + 3)
+
+    for r in range(1, 4):
+        copy_gp(r).start()
+    copy_gp_on(0).start()
     gps[own] = gp[...]
-    hid[own] = hidden[:, columns(own)]
-    each(team, lambda off: copy_gp(off).wait_recv())
-    each(team, lambda off: copy_hid(off).wait_recv())
+    for r in range(1, 4):
+        copy_gp(r).wait_recv()
+        copy_gp_on(r).start()
+    for r in range(4):
+        copy_gp_on(r).wait_recv()
     total = mm(hid[0], gps[0], 0, 0)
-    for i in range(1, team):
+    for i in range(1, 8):
         total = total + mm(hid[i], gps[i], 0, 0)
     part[...] = total.reshape(part.shape).astype(BF16)
-    each(half, lambda off: copy_part(off).start())
+    each(count, lambda off: copy_part(off).start())
     got[place] = part[place]
-    each(half, lambda off: copy_part(off).wait_recv())
+    each(count, lambda off: copy_part(off).wait_recv())
 
     def add(i, total):
         return total + got[i].astype(F32)
 
-    out[own, place] = lax.fori_loop(0, half, add, jnp.zeros(got.shape[1:], F32)).astype(BF16)
-    each(half, lambda off: copy_sum(off).start())
-    each(half, lambda off: copy_sum(off).wait_recv())
-    each(half, lambda off: copy_sum(off).wait_send())
-    each(team, lambda off: copy_team(off).start())
-    each(team, lambda off: copy_team(off).wait_recv())
-    each(team, lambda off: copy_team(off).wait_send())
-    each(team, lambda off: copy_gp(off).wait_send())
-    each(team, lambda off: copy_hid(off).wait_send())
-    each(half, lambda off: copy_part(off).wait_send())
+    out[own, place] = lax.fori_loop(0, count, add, jnp.zeros(got.shape[1:], F32)).astype(BF16)
+    each(count, lambda off: copy_sum(off).start())
+    for step in range(count + 2):
+        if step < count:
+            if step:
+                copy_sum(step).wait_recv()
+            for key in (1, 0, 3):
+                copy_on(key, step).start()
+        if 0 <= step - 1 < count:
+            copy_on(0, step - 1).wait_recv()
+            copy_on(2, step - 1).start()
+            copy_on(4, step - 1).start()
+            copy_on(1, step - 1).wait_recv()
+            copy_on(5, step - 1).start()
+        if step >= 2:
+            copy_on(2, step - 2).wait_recv()
+            copy_on(6, step - 2).start()
+    for off in range(count):
+        for key in range(7):
+            if key > 2:
+                copy_on(key, off).wait_recv()
+            copy_on(key, off).wait_send()
+    each(count, lambda off: copy_sum(off).wait_send())
+    each(count, lambda off: copy_part(off).wait_send())
+    for r in range(4):
+        if r:
+            copy_gp(r).wait_send()
+        copy_gp_on(r).wait_send()
 
 
 def call(kernel, ins, outs, scratch=(), collective=None):
@@ -345,14 +434,22 @@
     )(*ins)
 
 
-def scan(state, n, backward):
-    slices = state.reshape(n, -1, 128)
-    sems = [pltpu.SemaphoreType.DMA((n,))] * 4
-    (out,) = call(
-        functools.partial(scan_kernel, n, backward), [slices], [(slices.shape, BF16)],
-        [pltpu.VMEM(slices.shape, BF16)] * 2 + sems, collective=1 if backward else 0,
-    )
-    return out.reshape(-1, 128)
+def scan(state, n, hidden=None):
+    half = n // 2
+    halves = state.reshape(2, half, -1, 128)
+    ins, outs = [halves], [(halves.shape, BF16)]
+    sem = pltpu.SemaphoreType.DMA
+    sems = [sem((1,))] * 2 + [sem((half,))] * 6
+    if hidden is not None:
+        ins.append(hidden)
+        outs.append(((8, hidden.shape[0], hidden.shape[1] // 8), BF16))
+        sems = sems + [sem((8,))] * 2
+    scratch = [pltpu.VMEM(halves.shape[1:], BF16)] * 4 + [pltpu.VMEM(halves.shape, BF16)]
+    out, *rest = call(
+        functools.partial(scan_kernel, n, hidden is None), ins, outs, scratch + sems,
+        collective=1 if hidden is None else 0,
+    )
+    return out.reshape(-1, 128), *rest
 
 
 def shifted(array, axis, by):
@@ -361,7 +458,7 @@
     return lax.ppermute(array, axis, pairs)
 
 
-def body(n, dps, hidden_in, qk_weight, conv_weight, values, gate_in, cotangent):
+def body(n, hidden_in, qk_weight, conv_weight, values, gate_in, cotangent):
     tokens, v, gate, cot = hidden_in[0], values[0], gate_in[0], cotangent[0]
     length, depth = tokens.shape
     cols = qk_weight.shape[1]
@@ -376,7 +473,7 @@
     mixed, own = call(
         key_kernel, [projected, prev, conv_weight, v, *tables], [((length, cols), F32), state_shape]
     )
-    before = scan(own, n, False)
+    before, hid = scan(own, n, tokens)
     out, ggate, own_grad, dq, dk, dv = call(
         query_kernel,
         [mixed, v, gate, cot, before, *tables],
@@ -385,7 +482,7 @@
             ((length, cols // 2), F32), ((length, cols // 2), F32), ((length, wide), F32),
         ],
     )
-    after = scan(own_grad, n, True)
+    (after,) = scan(own_grad, n)
     gv, gm = call(
         value_kernel, [mixed, v, after, dq, dk, dv, *tables],
         [((length, wide), BF16), ((length, cols), F32)],
@@ -395,19 +492,17 @@
         hidden_kernel, [gm, later, conv_weight, qk_weight],
         [((length, cols), BF16), ((length, depth), BF16)],
     )
-    team, half = 2 * dps, n // 2
-    piece = depth // (team * half)
+    count = n // 4
+    piece = depth // (8 * count)
     sem = pltpu.SemaphoreType.DMA
     (gw,) = call(
-        functools.partial(weight_kernel, n, dps), [gp, tokens],
-        [((team, half, piece, cols), BF16)],
+        functools.partial(weight_kernel, n), [gp, hid], [((8, count, piece, cols), BF16)],
         [
-            pltpu.VMEM((team, length, cols), BF16),
-            pltpu.VMEM((team, length, depth // team), BF16),
-            pltpu.VMEM((half, piece, cols), BF16),
-            pltpu.VMEM((half, piece, cols), BF16),
+            pltpu.VMEM((8, length, cols), BF16),
+            pltpu.VMEM((count, piece, cols), BF16),
+            pltpu.VMEM((count, piece, cols), BF16),
         ]
-        + [sem((team,))] * 4 + [sem((half,))] * 4 + [sem((team,))] * 2,
+        + [sem((4,))] * 4 + [sem((count,))] * 4 + [sem((7, count))] * 2,
         collective=2,
     )
     return out[None], gh[None], gv[None], ggate[None], gw.reshape(depth, cols)
@@ -416,7 +511,7 @@
 def solution(mesh):
     split = P("dp", "ctx", None)
     return jax.shard_map(
-        functools.partial(body, mesh.shape["ctx"], mesh.shape["dp"]),
+        functools.partial(body, mesh.shape["ctx"]),
         mesh=mesh,
         in_specs=(split, P(), P(), split, split, split),
         out_specs=(split, split, split, split, P()),

time: 95.5 us -> 87.1 us (0.912); the launches traced: 93.8 us -> 86.9 us
  Pallas kernels: 83.9 us -> 77 us
    pallas_call x7, Pallas kernels: 83.9 us -> 77 us  [call(): pl.pallas_call(kernel, out_shape=[jax.ShapeDtypeStruct(s, t) for s, t in...]
where the time goes in v3:
time: 87.1 us; the launch traced here: 86.9 us
  Pallas kernels  77 us (88%)
  starting transfers between devices  3.64 us (4%)
  waiting for transfers between devices  2.57 us (3%)
  matrix products  1.78 us (2%)
  local copies, waits for them, and re-layouts  1.03 us (1%)
    pallas_call x7, Pallas kernels, call(): pl.pallas_call(kernel, out_shape=[jax.ShapeDtypeStruct(s, t) for s, t in...  77 us
    ppermute x2, starting transfers between devices, shifted(): return lax.ppermute(array, axis, pairs)  3.64 us
    ppermute x2, waiting for transfers between devices, shifted(): return lax.ppermute(array, axis, pairs)  2.57 us
    dot_general x1, matrix products, body(): jnp.dot(tokens, qk_weight, preferred_element_type=F32).astype(BF16)  1.78 us
  transfers between devices with their start and end apart: 2, of which 2 were waited for; matrix products, arithmetic and copies ran while one was open for 0% of the time, Pallas kernels for 0%

profile of v3, /device:TPU:0, one launch (start us, length us, event | category | flops | bytes accessed | tf_op | source)
XLA Modules:
  0.0 86.9 jit_solution(10231430877728154323)
XLA Ops:
  0.6 0.0 copy-start
  0.6 0.0 copy-start.1
  0.7 0.0 copy-start.4
  0.7 0.0 copy-start.5
  0.7 1.8 %convolution_convert_fusion.proj = bf16[128,256]{1,0:T(8,128)(2,1)S(1)} fusion(bf16[2048,256]{1,0:T(8,128)(2,1)} %weight.1, bf16[1,128,2048]{2,1,0:T(8,128)(2,1)} %param.9), kind=kOutput, calls=%fused_computation | convolution fusion | flops 134250496 | bytes 1638400 | tf_op jit(solution)/shard_map/dot_general | solution.py:471
  2.5 0.0 copy-start.8
  2.5 2.4 %collective-permute-start = (bf16[8,256]{1,0:T(8,128)(2,1)S(1)}, bf16[8,256]{1,0:T(8,128)(2,1)S(1)}, u32[]{:S(2)}, u32[]{:S(2)}) collective-permute-start(bf16[8,256]{1,0:T(8,128)(2,1)S(1)} %slice.8), channel_id=1, source_target_pairs={{0,1},{1,2},{2,3},{3,4},{4,5},{5,6},{6,7},{7,8},{8,9},{9,10},{10,1... | collective-permute-start | bytes 12296 | tf_op jit(solution)/shard_map/ppermute | solution.py:458
  4.9 0.8 collective-permute-done
  5.7 0.0 copy-done
  5.7 0.0 copy-done.1
  5.7 0.0 copy-done.4
  5.7 0.0 copy-done.5
  5.7 0.0 copy-done.8
  5.7 0.0 copy-start.3
  5.7 1.5 %shard_map.128 = (f32[128,256]{1,0:T(8,128)S(1)}, bf16[768,128]{1,0:T(8,128)(2,1)S(1)}) custom-call(bf16[128,256]{1,0:T(8,128)(2,1)S(1)} %convolution_convert_fusion.proj, f32[8,256]{1,0:T(8,128)S(1)} %convert_element_type.7.prev, f32[3,256]{1,0:T(4,128)S(1)} %copy-done.8, bf16[128,512]{1,0:T(8,128)(2,1)S(1)} %bitcast.18, bf16[128,2048]{1,0:T(8,128)(2,1)S(1)} %copy-done.1, ...), custom_call_target="tpu_custom_call" | custom-call | tf_op jit(solution)/shard_map/pallas_call | solution.py:427
  7.2 0.0 copy-done.3
  7.2 0.0 copy-start.6
  7.2 0.0 copy-start.7
  7.3 22.3 %shard_map.129 = (bf16[2,8,48,128]{3,2,1,0:T(8,128)(2,1)S(1)}, bf16[8,128,256]{2,1,0:T(8,128)(2,1)S(1)}) custom-call(bf16[2,8,48,128]{3,2,1,0:T(8,128)(2,1)S(1)} %bitcast.24, bf16[128,2048]{1,0:T(8,128)(2,1)S(1)} %bitcast.17), custom_call_target="tpu_custom_call" | custom-call | tf_op jit(solution)/shard_map/pallas_call | solution.py:427
  29.5 0.0 copy-done.6
  29.5 0.0 copy-done.7
  29.5 5.4 %shard_map.130 = (bf16[128,512]{1,0:T(8,128)(2,1)}, bf16[128,512]{1,0:T(8,128)(2,1)}, bf16[768,128]{1,0:T(8,128)(2,1)S(1)}, f32[128,128]{1,0:T(8,128)S(1)}, f32[...) custom-call(f32[128,256]{1,0:T(8,128)S(1)} %get-tuple-element.19.mixed, bf16[128,512]{1,0:T(8,128)(2,1)S(1)} %bitcast.19, ...), custom_call_target="tpu_custom_call" | custom-call | tf_op jit(solution)/shard_map/pallas_call | solution.py:427
  34.9 13.9 %shard_map.131 = bf16[2,8,48,128]{3,2,1,0:T(8,128)(2,1)S(1)} custom-call(bf16[2,8,48,128]{3,2,1,0:T(8,128)(2,1)S(1)} %bitcast.23), custom_call_target="tpu_custom_call" | custom-call | tf_op jit(solution)/shard_map/pallas_call | solution.py:427
  48.8 0.0 copy-start.2
  48.8 2.5 %shard_map.132 = (bf16[128,512]{1,0:T(8,128)(2,1)}, f32[128,256]{1,0:T(8,128)S(1)}) custom-call(f32[128,256]{1,0:T(8,128)S(1)} %get-tuple-element.19.mixed, bf16[128,512]{1,0:T(8,128)(2,1)S(1)} %bitcast.20, bf16[768,128]{1,0:T(8,128)(2,1)S(1)} %bitcast.21, f32[128,128]{1,0:T(8,128)S(1)} %get-tuple-element.24.dq_in, f32[128,128]{1,0:T(8,128)S(1)} %get-tuple-element.25.dk_in, ...), custom_call_target="tpu_custom_call" | custom-call | tf_op jit(solution)/shard_map/pallas_call | solution.py:427
  51.3 1.3 %collective-permute-start.1 = (f32[8,256]{1,0:T(8,128)S(1)}, f32[8,256]{1,0:T(8,128)S(1)}, u32[]{:S(2)}, u32[]{:S(2)}) collective-permute-start(f32[8,256]{1,0:T(8,128)S(1)} %slice.7), channel_id=1, source_target_pairs={{1,0},{2,1},{3,2},{4,3},{5,4},{6,5},{7,6},{8,7},{9,8},{10,9},{11,1... | collective-permute-start | bytes 24584 | tf_op jit(solution)/shard_map/ppermute | solution.py:458
  52.6 1.8 %collective-permute-done.1.later = f32[8,256]{1,0:T(8,128)S(1)} collective-permute-done((f32[8,256]{1,0:T(8,128)S(1)}, f32[8,256]{1,0:T(8,128)S(1)}, u32[]{:S(2)}, u32[]{:S(2)}) %collective-permute-start.1) | collective-permute-done | bytes 8224 | tf_op jit(solution)/shard_map/ppermute | solution.py:458
  54.4 0.0 copy-done.2
  54.4 1.3 %shard_map.133 = (bf16[128,256]{1,0:T(8,128)(2,1)S(1)}, bf16[128,2048]{1,0:T(8,128)(2,1)}) custom-call(f32[128,256]{1,0:T(8,128)S(1)} %get-tuple-element.27.gm, f32[8,256]{1,0:T(8,128)S(1)} %collective-permute-done.1.later, f32[3,256]{1,0:T(4,128)S(1)} %copy-done.8, bf16[2048,256]{1,0:T(8,128)(2,1)S(1)} %copy-done.2), custom_call_target="tpu_custom_call" | custom-call | tf_op jit(solution)/shard_map/pallas_call | solution.py:427
  55.7 30.2 %shard_map.134 = bf16[8,4,64,256]{3,2,1,0:T(8,128)(2,1)S(1)} custom-call(bf16[128,256]{1,0:T(8,128)(2,1)S(1)} %get-tuple-element.31.gp, bf16[8,128,256]{2,1,0:T(8,128)(2,1)S(1)} %get-tuple-element.32.hid), custom_call_target="tpu_custom_call" | custom-call | tf_op jit(solution)/shard_map/pallas_call | solution.py:427
  85.9 1.0 %copy.15 = bf16[2048,256]{1,0:T(8,128)(2,1)} copy(bf16[2048,256]{1,0:T(8,128)(2,1)S(1)} %bitcast.16) | data formatting | bytes 2097152
  (3 shorter events, 0.0 us)
Async XLA Ops:
  0.6 5.0 %copy-start = (bf16[128,2048]{1,0:T(8,128)(2,1)S(1)}, bf16[128,2048]{1,0:T(8,128)(2,1)}, u32[]{:S(2)}) copy-start(bf16[128,2048]{1,0:T(8,128)(2,1)} %constant.7.clone.second) | copy-start | bytes 1572868
  0.6 5.0 %copy-start.1 = (bf16[128,2048]{1,0:T(8,128)(2,1)S(1)}, bf16[128,2048]{1,0:T(8,128)(2,1)}, u32[]{:S(2)}) copy-start(bf16[128,2048]{1,0:T(8,128)(2,1)} %constant.6.clone.first) | copy-start | bytes 1572868
  0.7 5.0 %copy-start.4 = (bf16[1,128,512]{2,1,0:T(8,128)(2,1)S(1)}, bf16[1,128,512]{2,1,0:T(8,128)(2,1)}, u32[]{:S(2)}) copy-start(bf16[1,128,512]{2,1,0:T(8,128)(2,1)} %param.12) | copy-start | bytes 393220
  0.7 5.0 %copy-start.5 = (f32[8,2048]{1,0:T(8,128)S(1)}, f32[8,2048]{1,0:T(8,128)}, u32[]{:S(2)}) copy-start(f32[8,2048]{1,0:T(8,128)} %constant.8.clone.rows) | copy-start | bytes 196612
  2.5 3.2 %copy-start.8 = (f32[3,256]{1,0:T(4,128)S(1)}, f32[3,256]{1,0:T(4,128)}, u32[]{:S(2)}) copy-start(f32[3,256]{1,0:T(4,128)} %conv.3) | copy-start | bytes 9220
  2.5 3.2 %collective-permute-start = (bf16[8,256]{1,0:T(8,128)(2,1)S(1)}, bf16[8,256]{1,0:T(8,128)(2,1)S(1)}, u32[]{:S(2)}, u32[]{:S(2)}) collective-permute-start(bf16[8,256]{1,0:T(8,128)(2,1)S(1)} %slice.8), channel_id=1, source_target_pairs={{0,1},{1,2},{2,3},{3,4},{4,5},{5,6},{6,7},{7,8},{8,9},{9,10},{10,1... | collective-permute-start | bytes 12296 | tf_op jit(solution)/shard_map/ppermute | solution.py:458
  5.7 1.5 %copy-start.3 = (bf16[1,128,2048]{2,1,0:T(8,128)(2,1)S(1)}, bf16[1,128,2048]{2,1,0:T(8,128)(2,1)}, u32[]{:S(2)}) copy-start(bf16[1,128,2048]{2,1,0:T(8,128)(2,1)} %param.9) | copy-start | bytes 1572868
  7.2 22.3 %copy-start.6 = (bf16[1,128,512]{2,1,0:T(8,128)(2,1)S(1)}, bf16[1,128,512]{2,1,0:T(8,128)(2,1)}, u32[]{:S(2)}) copy-start(bf16[1,128,512]{2,1,0:T(8,128)(2,1)} %param.13) | copy-start | bytes 393220
  7.2 22.3 %copy-start.7 = (bf16[1,128,512]{2,1,0:T(8,128)(2,1)S(1)}, bf16[1,128,512]{2,1,0:T(8,128)(2,1)}, u32[]{:S(2)}) copy-start(bf16[1,128,512]{2,1,0:T(8,128)(2,1)} %param.14) | copy-start | bytes 393220
  48.8 5.6 %copy-start.2 = (bf16[2048,256]{1,0:T(8,128)(2,1)S(1)}, bf16[2048,256]{1,0:T(8,128)(2,1)}, u32[]{:S(2)}) copy-start(bf16[2048,256]{1,0:T(8,128)(2,1)} %weight.1) | copy-start | bytes 3145732
  51.3 3.1 %collective-permute-start.1 = (f32[8,256]{1,0:T(8,128)S(1)}, f32[8,256]{1,0:T(8,128)S(1)}, u32[]{:S(2)}, u32[]{:S(2)}) collective-permute-start(f32[8,256]{1,0:T(8,128)S(1)} %slice.7), channel_id=1, source_target_pairs={{1,0},{2,1},{3,2},{4,3},{5,4},{6,5},{7,6},{8,7},{9,8},{10,9},{11,1... | collective-permute-start | bytes 24584 | tf_op jit(solution)/shard_map/ppermute | solution.py:458

commit v4 on v3

--- a/solution.py
+++ b/solution.py
@@ -76,13 +76,16 @@
         ref[NORM_ROW + 16 :, :] = jnp.zeros((rest, 128), BF16)
 
 
-def key_kernel(proj, prev, conv, values, first, second, rows, mixed_out, state_out):
+def mix(proj, prev, conv, mixed_out):
     length = proj.shape[0]
-    padded = jnp.concatenate([prev[...], proj[...].astype(F32)], 0)
+    padded = jnp.concatenate([prev[8:, :].astype(F32), proj[...].astype(F32)], 0)
     mixed = conv[0:1, :] * padded[8 : 8 + length]
     for j in range(1, KCONV):
         mixed = mixed + conv[j : j + 1, :] * padded[8 - j : 8 - j + length]
     mixed_out[...] = mixed
+
+
+def key_part(mixed, values, first, second, rows, state_out):
     keys = mixed[:, H * F :].astype(BF16)
     states, norms = [], []
     for h in range(H):
@@ -93,7 +96,7 @@
     store_state(state_out, states, norms)
 
 
-def query_kernel(
+def query_part(
     mixed, values, gate, cot, state, first, second, rows, out, ggate, state_out, dq_out, dk_out, dv_out
 ):
     length = mixed.shape[0]
@@ -156,7 +159,7 @@
     dk_out[...] = dk
 
 
-def value_kernel(mixed, values, state, dq_in, dk_in, dv_in, first, second, rows, gv, gm):
+def value_part(mixed, values, state, dq_in, dk_in, dv_in, first, second, rows, gv, gm):
     keys = mixed[:, H * F :].astype(BF16)
     incoming = state[...]
     norm_rows = incoming[NORM_ROW : NORM_ROW + 16].astype(F32)
@@ -179,15 +182,13 @@
     gm[:, H * F :] = dk
 
 
-def hidden_kernel(gm, later, conv, weight, gp_out, gh):
+def project_back(gm, later, conv, gp_out):
     length = gm.shape[0]
     extended = jnp.concatenate([gm[...], later[...]], 0)
     gp = conv[0:1, :] * extended[0:length]
     for j in range(1, KCONV):
         gp = gp + conv[j : j + 1, :] * extended[j : j + length]
-    gp = gp.astype(BF16)
-    gp_out[...] = gp
-    gh[...] = mm(gp, weight[...], 1, 1).astype(BF16)
+    gp_out[...] = gp.astype(BF16)
 
 
 def remote(src, dst, s, r, device):
@@ -213,21 +214,12 @@
     )
 
 
-def scan_kernel(n, backward, *refs):
-    if backward:
-        state, out, theirs, both, got, sums, give, *sems = refs
-        team = 1
-    else:
-        state, hidden, out, hid, theirs, both, got, sums, give, *sems = refs
-        team = 8
-        width = hidden.shape[1] // team
-        sh, rh = sems[8:]
-    s0, r0, s1, r1, s2, r2, s3, r3 = sems[:8]
+def scan_part(n, backward, state, out, theirs, both, got, sums, give, s0, r0, s1, r1, s2, r2, s3, r3):
     dp, me = lax.axis_index("dp"), lax.axis_index("ctx")
     core, pair = lax.rem(me, 2), me // 2
     half = n // 2
+    size = got.shape[1]
     other = (dp, pair * 2 + 1 - core)
-    mine = dp * 4 + lax.rem(me, 4)
 
     def peer(off):
         return lax.rem(pair + off, half)
@@ -238,47 +230,29 @@
     def far(off):
         return (dp, peer(off) * 2 + core)
 
-    def mate(off):
-        return lax.rem(mine + off, team)
-
-    def member(i):
-        return (i // 4, me // 4 * 4 + lax.rem(i, 4))
-
-    def columns(i):
-        return pl.ds(pl.multiple_of(i * width, width), width)
+    def part(at, count=1):
+        return pl.ds(pl.multiple_of(at * size, 16), count * size)
 
     def copy0():
-        return remote(state.at[1 - core], theirs, s0.at[0], r0.at[0], other)
+        return remote(state.at[part((1 - core) * half, half)], theirs, s0.at[0], r0.at[0], other)
 
     def copy1(off):
-        return remote(both.at[peer(off)], got.at[pair], s1.at[off], r1.at[off], far(off))
+        return remote(both.at[part(peer(off))], got.at[pair], s1.at[off], r1.at[off], far(off))
 
     def copy2(off):
         return remote(sums.at[peer(off)], give.at[0, pair], s2.at[off], r2.at[off], far(off))
 
     def copy3(off):
         at = slot(off)
-        return remote(give.at[1, at], out.at[core, at], s3.at[off], r3.at[off], other)
-
-    def copy_hid(off):
         return remote(
-            hidden.at[:, columns(mate(off))], hid.at[mine], sh.at[off], rh.at[off], member(mate(off))
+            give.at[1, at], out.at[part(core * half + at)], s3.at[off], r3.at[off], other
         )
 
-    barrier = pltpu.get_barrier_semaphore()
-    greet(other)
-    each(half, lambda off: greet(far(off)))
-    each(team, lambda off: greet(member(mate(off))))
-    pl.semaphore_wait(barrier, half + team - 1)
-
     copy0().start()
-    each(team, lambda off: copy_hid(off).start())
-    if team > 1:
-        hid[mine] = hidden[:, columns(mine)]
     copy0().wait_recv()
-    both[...] = (state[core].astype(F32) + theirs[...].astype(F32)).astype(BF16)
+    both[...] = (state[part(core * half, half)].astype(F32) + theirs[...].astype(F32)).astype(BF16)
     each(half, lambda off: copy1(off).start())
-    got[pair] = both[pair]
+    got[pair] = both[part(pair)]
     each(half, lambda off: copy1(off).wait_recv())
 
     def add(i, total):
@@ -296,9 +270,10 @@
     def hand_on(off):
         at = slot(off)
         before = give[0, at].astype(F32)
-        out[core, at] = (before + mine_late * theirs[at].astype(F32)).astype(BF16)
-        give[1, at] = (before + other_late * state[core, at].astype(F32)).astype(BF16)
+        own = part(core * half + at)
+        give[1, at] = (before + other_late * state[own].astype(F32)).astype(BF16)
         copy3(off).start()
+        out[own] = (before + mine_late * theirs[part(at)].astype(F32)).astype(BF16)
 
     def arrive(off):
         copy2(off).wait_recv()
@@ -307,19 +282,33 @@
     hand_on(0)
     each(half, arrive)
     each(half, lambda off: copy3(off).wait_recv(), 0)
-    each(half, lambda off: copy3(off).wait_send(), 0)
-    each(half, lambda off: copy2(off).wait_send())
-    each(half, lambda off: copy1(off).wait_send())
-    copy0().wait_send()
-    each(team, lambda off: copy_hid(off).wait())
-
-
-def weight_kernel(n, gp, hid, out, gps, part, got, sa, ra, sb, rb, sc, rc, sd, rd, se, re):
+
+    def finish():
+        each(half, lambda off: copy3(off).wait_send(), 0)
+        each(half, lambda off: copy2(off).wait_send())
+        each(half, lambda off: copy1(off).wait_send())
+        copy0().wait_send()
+
+    return finish
+
+
+def layer_kernel(n, *refs):
+    hidden, weight, conv, values, gate, cot, first, second, rows = refs[:9]
+    out, gh, gv, ggate, gw = refs[9:14]
+    proj, prev, later, mixed, state, before, grad_state, after = refs[14:22]
+    dq, dk, dv, gm, gp, hid, gps, part, got = refs[22:31]
+    scan1, scan2 = refs[31:36], refs[36:41]
+    sems1, sems2 = refs[41:49], refs[49:57]
+    sh, rh, halo, sa, ra, sb, rb, sc, rc, sd, rd, se, re = refs[57:]
+    tables = (first, second, rows)
+    length = hidden.shape[0]
+
     dp, me = lax.axis_index("dp"), lax.axis_index("ctx")
     count = n // 4
     place, sub = me // 4, lax.rem(me, 4)
     row, core = sub // 2, lax.rem(sub, 2)
     own = dp * 4 + sub
+    width = hid.shape[2]
 
     def peer(off):
         return lax.rem(place + off, count)
@@ -344,6 +333,26 @@
     other = (dp, place * 4 + row * 2 + 1 - core)
     sides = [(0, 0), (0, 1), (1, 0), (1, 1)]
 
+    def mate(off):
+        return lax.rem(own + off, 8)
+
+    def member(i):
+        return (i // 4, place * 4 + lax.rem(i, 4))
+
+    def columns(i):
+        return pl.ds(pl.multiple_of(i * width, width), width)
+
+    def copy_hid(off):
+        return remote(
+            hidden.at[:, columns(mate(off))], hid.at[own], sh.at[off], rh.at[off], member(mate(off))
+        )
+
+    def copy_prev():
+        return remote(proj.at[pl.ds(length - 16, 16)], prev, halo.at[0], halo.at[1], (dp, me + 1))
+
+    def copy_later():
+        return remote(gm.at[pl.ds(0, 8)], later, halo.at[2], halo.at[3], (dp, me - 1))
+
     def copy_gp(r):
         return remote(gp, gps.at[own], sa.at[r], ra.at[r], device(*sides[r]))
 
@@ -355,27 +364,63 @@
         return remote(part.at[peer(off)], got.at[place], sc.at[off], rc.at[off], far(off))
 
     def copy_sum(off):
-        ref = out.at[own, place]
+        ref = gw.at[own, place]
         return remote(ref, ref, sd.at[off], rd.at[off], far(off))
 
     def copy_on(key, off):
-        first, second = ((0, 1), (1, 0)) if off % 2 == 0 else ((1, 0), (0, 1))
-        source = ((0, 0), (0, 0), first, (0, 0), first, second, (1, 1))[key]
-        target = other if key > 2 else device(*(first if key == 0 else second))
-        ref = out.at[ident(*source), slot(off)]
+        one, two = ((0, 1), (1, 0)) if off % 2 == 0 else ((1, 0), (0, 1))
+        source = ((0, 0), (0, 0), one, (0, 0), one, two, (1, 1))[key]
+        target = other if key > 2 else device(*(one if key == 0 else two))
+        ref = gw.at[ident(*source), slot(off)]
         return remote(ref, ref, se.at[key, off], re.at[key, off], target)
 
     barrier = pltpu.get_barrier_semaphore()
-    greet(other)
-    for r in range(1, 4):
-        greet(device(*sides[r]))
-    each(count, lambda off: greet(far(off)))
-    pl.semaphore_wait(barrier, count + 3)
-
+    each(n, lambda off: greet((dp, lax.rem(me + off, n))))
+    each(4, lambda i: greet((1 - dp, place * 4 + i)), 0)
+    proj[...] = mm(hidden[...], weight[...]).astype(BF16)
+    pl.semaphore_wait(barrier, n + 3)
+
+    @pl.when(me < n - 1)
+    def _():
+        copy_prev().start()
+
+    each(8, lambda off: copy_hid(off).start())
+    hid[own] = hidden[:, columns(own)]
+
+    @pl.when(me > 0)
+    def _():
+        copy_prev().wait_recv()
+
+    @pl.when(me == 0)
+    def _():
+        prev[...] = jnp.zeros(prev.shape, BF16)
+
+    mix(proj, prev, conv, mixed)
+    key_part(mixed, values, *tables, state)
+    finish1 = scan_part(n, False, state, before, *scan1, *sems1)
+    query_part(mixed, values, gate, cot, before, *tables, out, ggate, grad_state, dq, dk, dv)
+    finish2 = scan_part(n, True, grad_state, after, *scan2, *sems2)
+    value_part(mixed, values, after, dq, dk, dv, *tables, gv, gm)
+
+    @pl.when(me > 0)
+    def _():
+        copy_later().start()
+
+    @pl.when(me < n - 1)
+    def _():
+        copy_later().wait_recv()
+
+    @pl.when(me == n - 1)
+    def _():
+        later[...] = jnp.zeros(later.shape, F32)
+
+    project_back(gm, later, conv, gp)
     for r in range(1, 4):
         copy_gp(r).start()
     copy_gp_on(0).start()
     gps[own] = gp[...]
+    gh[...] = mm(gp[...], weight[...], 1, 1).astype(BF16)
+    each(8, lambda off: copy_hid(off).wait_recv())
     for r in range(1, 4):
         copy_gp(r).wait_recv()
         copy_gp_on(r).start()
@@ -392,7 +437,7 @@
     def add(i, total):
         return total + got[i].astype(F32)
 
-    out[own, place] = lax.fori_loop(0, count, add, jnp.zeros(got.shape[1:], F32)).astype(BF16)
+    gw[own, place] = lax.fori_loop(0, count, add, jnp.zeros(got.shape[1:], F32)).astype(BF16)
     each(count, lambda off: copy_sum(off).start())
     for step in range(count + 2):
         if step < count:
@@ -420,42 +465,17 @@
         if r:
             copy_gp(r).wait_send()
         copy_gp_on(r).wait_send()
-
-
-def call(kernel, ins, outs, scratch=(), collective=None):
-    extra = {} if collective is None else dict(collective_id=collective, has_side_effects=True)
-    return pl.pallas_call(
-        kernel,
-        out_shape=[jax.ShapeDtypeStruct(s, t) for s, t in outs],
-        in_specs=[VM] * len(ins),
-        out_specs=[VM] * len(outs),
-        scratch_shapes=list(scratch),
-        compiler_params=pltpu.CompilerParams(vmem_limit_bytes=48 * 2**20, **extra),
-    )(*ins)
-
-
-def scan(state, n, hidden=None):
-    half = n // 2
-    halves = state.reshape(2, half, -1, 128)
-    ins, outs = [halves], [(halves.shape, BF16)]
-    sem = pltpu.SemaphoreType.DMA
-    sems = [sem((1,))] * 2 + [sem((half,))] * 6
-    if hidden is not None:
-        ins.append(hidden)
-        outs.append(((8, hidden.shape[0], hidden.shape[1] // 8), BF16))
-        sems = sems + [sem((8,))] * 2
-    scratch = [pltpu.VMEM(halves.shape[1:], BF16)] * 4 + [pltpu.VMEM(halves.shape, BF16)]
-    out, *rest = call(
-        functools.partial(scan_kernel, n, hidden is None), ins, outs, scratch + sems,
-        collective=1 if hidden is None else 0,
-    )
-    return out.reshape(-1, 128), *rest
-
-
-def shifted(array, axis, by):
-    length = lax.axis_size(axis)
-    pairs = [(i, i + by) for i in range(length) if 0 <= i + by < length]
-    return lax.ppermute(array, axis, pairs)
+    finish1()
+    finish2()
+    each(8, lambda off: copy_hid(off).wait_send())
+
+    @pl.when(me < n - 1)
+    def _():
+        copy_prev().wait_send()
+
+    @pl.when(me > 0)
+    def _():
+        copy_later().wait_send()
 
 
 def body(n, hidden_in, qk_weight, conv_weight, values, gate_in, cotangent):
@@ -464,46 +484,42 @@
     cols = qk_weight.shape[1]
     wide = v.shape[1]
     first, second, rows = feature_tables()
-    tables = [jnp.asarray(first, BF16), jnp.asarray(second, BF16), jnp.asarray(rows)]
-    state_rows = n * 16 * -(-(NORM_ROW + 16) // (16 * n))
-    state_shape = ((state_rows, 128), BF16)
-
-    projected = jnp.dot(tokens, qk_weight, preferred_element_type=F32).astype(BF16)
-    prev = shifted(projected[length - 8 :], "ctx", 1).astype(F32)
-    mixed, own = call(
-        key_kernel, [projected, prev, conv_weight, v, *tables], [((length, cols), F32), state_shape]
-    )
-    before, hid = scan(own, n, tokens)
-    out, ggate, own_grad, dq, dk, dv = call(
-        query_kernel,
-        [mixed, v, gate, cot, before, *tables],
-        [
-            ((length, wide), BF16), ((length, wide), BF16), state_shape,
-            ((length, cols // 2), F32), ((length, cols // 2), F32), ((length, wide), F32),
-        ],
-    )
-    (after,) = scan(own_grad, n)
-    gv, gm = call(
-        value_kernel, [mixed, v, after, dq, dk, dv, *tables],
-        [((length, wide), BF16), ((length, cols), F32)],
-    )
-    later = shifted(gm[:8], "ctx", -1)
-    gp, gh = call(
-        hidden_kernel, [gm, later, conv_weight, qk_weight],
-        [((length, cols), BF16), ((length, depth), BF16)],
-    )
-    count = n // 4
+    half, count = n // 2, n // 4
+    size = 16 * -(-(NORM_ROW + 16) // (16 * n))
     piece = depth // (8 * count)
-    sem = pltpu.SemaphoreType.DMA
-    (gw,) = call(
-        functools.partial(weight_kernel, n), [gp, hid], [((8, count, piece, cols), BF16)],
-        [
-            pltpu.VMEM((8, length, cols), BF16),
-            pltpu.VMEM((count, piece, cols), BF16),
-            pltpu.VMEM((count, piece, cols), BF16),
+    sem, vmem = pltpu.SemaphoreType.DMA, pltpu.VMEM
+    state = vmem((n * size, 128), BF16)
+    scan = [
+        vmem((half * size, 128), BF16), vmem((half * size, 128), BF16),
+        vmem((half, size, 128), BF16), vmem((half, size, 128), BF16),
+        vmem((2, half, size, 128), BF16),
+    ]
+    scan_sems = [sem((1,))] * 2 + [sem((half,))] * 6
+    outs = [
+        ((length, wide), BF16), ((length, depth), BF16), ((length, wide), BF16),
+        ((length, wide), BF16), ((8, count, piece, cols), BF16),
+    ]
+    out, gh, gv, ggate, gw = pl.pallas_call(
+        functools.partial(layer_kernel, n),
+        out_shape=[jax.ShapeDtypeStruct(s, t) for s, t in outs],
+        in_specs=[VM] * 9,
+        out_specs=[VM] * 5,
+        scratch_shapes=[
+            vmem((length, cols), BF16), vmem((16, cols), BF16), vmem((8, cols), F32),
+            vmem((length, cols), F32), state, state, state, state,
+            vmem((length, cols // 2), F32), vmem((length, cols // 2), F32),
+            vmem((length, wide), F32), vmem((length, cols), F32), vmem((length, cols), BF16),
+            vmem((8, length, depth // 8), BF16), vmem((8, length, cols), BF16),
+            vmem((count, piece, cols), BF16), vmem((count, piece, cols), BF16),
         ]
-        + [sem((4,))] * 4 + [sem((count,))] * 4 + [sem((7, count))] * 2,
-        collective=2,
+        + scan * 2 + scan_sems * 2
+        + [sem((8,))] * 2 + [sem((4,))] * 5 + [sem((count,))] * 4 + [sem((7, count))] * 2,
+        compiler_params=pltpu.CompilerParams(
+            vmem_limit_bytes=48 * 2**20, collective_id=0, has_side_effects=True
+        ),
+    )(
+        tokens, qk_weight, conv_weight, v, gate, cot,
+        jnp.asarray(first, BF16), jnp.asarray(second, BF16), jnp.asarray(rows),
     )
     return out[None], gh[None], gv[None], ggate[None], gw.reshape(depth, cols)
 

time: 87.1 us -> 80.8 us (0.928)
  local copies, waits for them, and re-layouts: 1.03 us -> 12.3 us
  Pallas kernels: 77 us -> 67.4 us
  starting transfers between devices: 3.64 us -> 0 us
  waiting for transfers between devices: 2.57 us -> 0 us
  matrix products: 1.78 us -> 0 us
    unnamed x19 -> x23, local copies, waits for them, and re-layouts: 1.03 us -> 12.3 us
    pallas_call x7 -> x1, Pallas kernels: 77 us -> 67.4 us  [body(): pl.pallas_call(functools.partial(layer_kernel, n), out_shape=[jax.ShapeDt...]
    ppermute x2 -> x0, starting transfers between devices: 3.64 us -> none  [shifted(): return lax.ppermute(array, axis, pairs)]
    ppermute x2 -> x0, waiting for transfers between devices: 2.57 us -> none  [shifted(): return lax.ppermute(array, axis, pairs)]
    dot_general x1 -> x0, matrix products: 1.78 us -> none  [body(): jnp.dot(tokens, qk_weight, preferred_element_type=F32).astype(BF16)]
  transfers between devices with their start and end apart: 2 -> 0, of which waited for: 2 -> 0; matrix products, arithmetic and copies ran while one was open for 0% -> 0% of each run, Pallas kernels for 0% -> 0%
where the time goes in v4:
time: 80.8 us; the launch traced here: 80.4 us
  Pallas kernels  67.4 us (83%)
  local copies, waits for them, and re-layouts  12.3 us (15%)
    pallas_call x1, Pallas kernels, body(): pl.pallas_call(functools.partial(layer_kernel, n), out_shape=[jax.ShapeDt...  67.4 us
    unnamed x23, local copies, waits for them, and re-layouts  12.3 us

profile of v4, /device:TPU:0, one launch (start us, length us, event | category | flops | bytes accessed | tf_op | source)
XLA Modules:
  0.0 80.4 jit_solution(2768838276722432219)
XLA Ops:
  0.6 0.0 copy-start.8
  0.6 0.7 copy-done.8
  1.3 0.0 copy-start
  1.3 1.2 %copy-done = bf16[2048,256]{1,0:T(8,128)(2,1)S(1)} copy-done((bf16[2048,256]{1,0:T(8,128)(2,1)S(1)}, bf16[2048,256]{1,0:T(8,128)(2,1)}, u32[]{:S(2)}) %copy-start) | copy-done | bytes 1048600
  2.5 0.0 copy-start.1
  2.5 1.0 %copy-done.1 = bf16[1,128,2048]{2,1,0:T(8,128)(2,1)S(1)} copy-done((bf16[1,128,2048]{2,1,0:T(8,128)(2,1)S(1)}, bf16[1,128,2048]{2,1,0:T(8,128)(2,1)}, u32[]{:S(2)}) %copy-start.1) | copy-done | bytes 524312
  3.6 0.0 copy-start.2
  3.6 1.0 %copy-done.2 = bf16[128,2048]{1,0:T(8,128)(2,1)S(1)} copy-done((bf16[128,2048]{1,0:T(8,128)(2,1)S(1)}, bf16[128,2048]{1,0:T(8,128)(2,1)}, u32[]{:S(2)}) %copy-start.2) | copy-done | bytes 524312
  4.6 0.0 copy-start.3
  4.6 1.0 %copy-done.3 = bf16[128,2048]{1,0:T(8,128)(2,1)S(1)} copy-done((bf16[128,2048]{1,0:T(8,128)(2,1)S(1)}, bf16[128,2048]{1,0:T(8,128)(2,1)}, u32[]{:S(2)}) %copy-start.3) | copy-done | bytes 524312
  5.7 0.0 copy-start.4
  5.7 0.9 %copy-done.4 = bf16[1,128,512]{2,1,0:T(8,128)(2,1)S(1)} copy-done((bf16[1,128,512]{2,1,0:T(8,128)(2,1)S(1)}, bf16[1,128,512]{2,1,0:T(8,128)(2,1)}, u32[]{:S(2)}) %copy-start.4) | copy-done | bytes 131096
  6.6 0.0 copy-start.5
  6.6 0.9 %copy-done.5 = bf16[1,128,512]{2,1,0:T(8,128)(2,1)S(1)} copy-done((bf16[1,128,512]{2,1,0:T(8,128)(2,1)S(1)}, bf16[1,128,512]{2,1,0:T(8,128)(2,1)}, u32[]{:S(2)}) %copy-start.5) | copy-done | bytes 131096
  7.5 0.0 copy-start.6
  7.5 0.9 %copy-done.6 = bf16[1,128,512]{2,1,0:T(8,128)(2,1)S(1)} copy-done((bf16[1,128,512]{2,1,0:T(8,128)(2,1)S(1)}, bf16[1,128,512]{2,1,0:T(8,128)(2,1)}, u32[]{:S(2)}) %copy-start.6) | copy-done | bytes 131096
  8.4 0.0 copy-start.7
  8.4 0.8 %copy-done.7 = f32[8,2048]{1,0:T(8,128)S(1)} copy-done((f32[8,2048]{1,0:T(8,128)S(1)}, f32[8,2048]{1,0:T(8,128)}, u32[]{:S(2)}) %copy-start.7) | copy-done | bytes 65560
  9.2 67.4 %shard_map.128 = (bf16[128,512]{1,0:T(8,128)(2,1)S(1)}, bf16[128,2048]{1,0:T(8,128)(2,1)S(1)}, bf16[128,512]{1,0:T(8,128)(2,1)S(1)}, bf16[128,512]{1,0:T(8,128)(2,1)S(1)}, bf16[8,4,64,256]{3,2,1,0:T(8,128)(2,1)S(1)}) custom-call(bf16[128,2048]{1,0:T(8,128)(2,1)S(1)} %bitcast.11, bf16[2048,256]{1,0:T(8,128)(2,1)S(1)} %copy-done, f32[3,256]{1,0:T(4,128)S(1)} %copy-done.8, ...), custom_call_target="tpu_custom_call" | custom-call | tf_op jit(solution)/shard_map/pallas_call | solution.py:502
  76.6 0.7 copy.19
  77.3 0.8 copy.20
  78.1 0.7 copy.21
  78.7 0.7 copy.22
  79.4 1.0 %copy.23 = bf16[2048,256]{1,0:T(8,128)(2,1)} copy(bf16[2048,256]{1,0:T(8,128)(2,1)S(1)} %bitcast.9) | data formatting | bytes 2097152
Async XLA Ops:
  0.6 0.7 copy-start.8
  1.3 1.2 %copy-start = (bf16[2048,256]{1,0:T(8,128)(2,1)S(1)}, bf16[2048,256]{1,0:T(8,128)(2,1)}, u32[]{:S(2)}) copy-start(bf16[2048,256]{1,0:T(8,128)(2,1)} %refs_1_.1) | copy-start | bytes 3145732
  2.5 1.0 %copy-start.1 = (bf16[1,128,2048]{2,1,0:T(8,128)(2,1)S(1)}, bf16[1,128,2048]{2,1,0:T(8,128)(2,1)}, u32[]{:S(2)}) copy-start(bf16[1,128,2048]{2,1,0:T(8,128)(2,1)} %param.9) | copy-start | bytes 1572868
  3.6 1.0 %copy-start.2 = (bf16[128,2048]{1,0:T(8,128)(2,1)S(1)}, bf16[128,2048]{1,0:T(8,128)(2,1)}, u32[]{:S(2)}) copy-start(bf16[128,2048]{1,0:T(8,128)(2,1)} %constant.7.clone.refs_7_) | copy-start | bytes 1572868
  4.6 1.0 %copy-start.3 = (bf16[128,2048]{1,0:T(8,128)(2,1)S(1)}, bf16[128,2048]{1,0:T(8,128)(2,1)}, u32[]{:S(2)}) copy-start(bf16[128,2048]{1,0:T(8,128)(2,1)} %constant.6.clone.refs_6_) | copy-start | bytes 1572868
  5.7 0.9 %copy-start.4 = (bf16[1,128,512]{2,1,0:T(8,128)(2,1)S(1)}, bf16[1,128,512]{2,1,0:T(8,128)(2,1)}, u32[]{:S(2)}) copy-start(bf16[1,128,512]{2,1,0:T(8,128)(2,1)} %param.12) | copy-start | bytes 393220
  6.6 0.9 %copy-start.5 = (bf16[1,128,512]{2,1,0:T(8,128)(2,1)S(1)}, bf16[1,128,512]{2,1,0:T(8,128)(2,1)}, u32[]{:S(2)}) copy-start(bf16[1,128,512]{2,1,0:T(8,128)(2,1)} %param.13) | copy-start | bytes 393220
  7.5 0.9 %copy-start.6 = (bf16[1,128,512]{2,1,0:T(8,128)(2,1)S(1)}, bf16[1,128,512]{2,1,0:T(8,128)(2,1)}, u32[]{:S(2)}) copy-start(bf16[1,128,512]{2,1,0:T(8,128)(2,1)} %param.14) | copy-start | bytes 393220
  8.4 0.8 %copy-start.7 = (f32[8,2048]{1,0:T(8,128)S(1)}, f32[8,2048]{1,0:T(8,128)}, u32[]{:S(2)}) copy-start(f32[8,2048]{1,0:T(8,128)} %constant.8.clone.refs_8_) | copy-start | bytes 196612

commit v5 on v4

--- a/solution.py
+++ b/solution.py
@@ -61,19 +61,22 @@
     return jnp.concatenate([norms[h : h + 1], norms[tail : tail + 1]], 1)
 
 
-def store_state(ref, states, norms):
+def store_state(ref, states):
     for h in range(H):
         ref[h * DV : (h + 1) * DV, :] = states[h][:, :128].astype(BF16)
     for g in range(2):
         tail = sum(states[4 * g + i][:, 128:] for i in range(4))
         ref[H * DV + g * DV : H * DV + (g + 1) * DV, :] = tail.astype(BF16)
+    rest = ref.shape[0] - NORM_ROW
+    if rest:
+        ref[NORM_ROW:, :] = jnp.zeros((rest, 128), BF16)
+
+
+def norm_block(norms):
     rows = [norms[h][:, :128] for h in range(H)]
     rows += [sum(norms[4 * g + i][:, 128:] for i in range(4)) for g in range(2)]
     rows.append(jnp.zeros((16 - len(rows), 128), F32))
-    ref[NORM_ROW : NORM_ROW + 16, :] = jnp.concatenate(rows, 0).astype(BF16)
-    rest = ref.shape[0] - NORM_ROW - 16
-    if rest:
-        ref[NORM_ROW + 16 :, :] = jnp.zeros((rest, 128), BF16)
+    return jnp.concatenate(rows, 0)
 
 
 def mix(proj, prev, conv, mixed_out):
@@ -93,76 +96,116 @@
         phi = (mm(keys, first[:, at]) + rows[0:1, at]) * (mm(keys, second[:, at]) + rows[1:2, at])
         states.append(mm(head_slice(values, h), phi.astype(BF16), 0, 0))
         norms.append(jnp.sum(phi, 0, keepdims=True))
-    store_state(state_out, states, norms)
-
-
-def query_part(
-    mixed, values, gate, cot, state, first, second, rows, out, ggate, state_out, dq_out, dk_out, dv_out
-):
-    length = mixed.shape[0]
+    store_state(state_out, states)
+    return norm_block(norms)
+
+
+def heads_of(mixed):
+    lane = lax.broadcasted_iota(jnp.int32, (mixed.shape[0], H * F), 1) // F
     q = mixed[:, : H * F].astype(BF16)
     k = mixed[:, H * F :].astype(BF16)
-    lane = lax.broadcasted_iota(jnp.int32, (length, H * F), 1) // F
-    causal = lax.broadcasted_iota(jnp.int32, (length, length), 0) >= lax.broadcasted_iota(
+    zero = jnp.zeros_like(q)
+    return q, k, lambda a, h: jnp.where(lane == h, a, zero)
+
+
+def causal_of(length):
+    return lax.broadcasted_iota(jnp.int32, (length, length), 0) >= lax.broadcasted_iota(
         jnp.int32, (length, length), 1
     )
-    zero = jnp.zeros_like(q)
+
+
+def weights_of(s, causal):
+    return jnp.where(causal, 1.0 + s + 0.5 * s * s, 0.0)
+
+
+def local_part(mixed, values, first, second, rows, s_ref, num_ref, one_ref, two_ref):
+    q, k, only = heads_of(mixed)
+    causal = causal_of(mixed.shape[0])
+    for h in range(H):
+        at = slice(h * FP, (h + 1) * FP)
+        s = mm(only(q, h), k, 1, 1) * F**-0.5
+        s_ref[h] = s
+        num_ref[h] = mm(weights_of(s, causal).astype(BF16), head_slice(values, h))
+        one_ref[:, at] = mm(q, first[:, at]) + rows[0:1, at]
+        two_ref[:, at] = (mm(q, second[:, at]) + rows[1:2, at]) * rows[2:3, at]
+
+
+def denom_part(norm_rows, gate, cot, s_ref, one_ref, two_ref, ng_ref, inv_ref, state_out):
+    causal = causal_of(s_ref.shape[1])
+    states = []
+    for h in range(H):
+        at = slice(h * FP, (h + 1) * FP)
+        phi = one_ref[:, at] * two_ref[:, at]
+        den = jnp.sum(weights_of(s_ref[h], causal), 1, keepdims=True) + jnp.sum(
+            phi * head_norm(norm_rows, h), 1, keepdims=True
+        )
+        inv = 1.0 / den
+        g = head_slice(gate, h).astype(F32)
+        ga = head_slice(cot, h).astype(F32) * g / (1.0 + jnp.exp(-g))
+        ng = (ga * inv).astype(BF16)
+        inv_ref[h] = inv
+        ng_ref[h] = ng
+        states.append(mm(ng, phi.astype(BF16), 0, 0))
+    store_state(state_out, states)
+
+
+def attend_part(gate, cot, state, num_ref, one_ref, two_ref, inv_ref, gd_ref, out, ggate):
     incoming = state[...]
-    norm_rows = incoming[NORM_ROW : NORM_ROW + 16].astype(F32)
-    dq = jnp.zeros((length, H * F), F32)
-    dk = jnp.zeros((length, H * F), F32)
-    states, norms, outs, ggates, dvs = [], [], [], [], []
+    norms, outs, ggates = [], [], []
     for h in range(H):
         at = slice(h * FP, (h + 1) * FP)
-        first_h, second_h, scale = first[:, at], second[:, at], rows[2:3, at]
-        qh = jnp.where(lane == h, q, zero)
-        kh = jnp.where(lane == h, k, zero)
-        v = head_slice(values, h)
-        s = mm(qh, k, 1, 1) * F**-0.5
-        w = jnp.where(causal, 1.0 + s + 0.5 * s * s, 0.0)
-        w16 = w.astype(BF16)
-        one = mm(q, first_h) + rows[0:1, at]
-        two = (mm(q, second_h) + rows[1:2, at]) * scale
-        phi = one * two
-        phi16 = phi.astype(BF16)
-        state_h = head_state(incoming, h)
-        norm_h = head_norm(norm_rows, h)
-        den = jnp.sum(w, 1, keepdims=True) + jnp.sum(phi * norm_h, 1, keepdims=True)
-        inv = 1.0 / den
-        att = (mm(w16, v) + mm(phi16, state_h, 1, 1)) * inv
+        phi = one_ref[:, at] * two_ref[:, at]
+        inv = inv_ref[h]
+        att = (num_ref[h] + mm(phi.astype(BF16), head_state(incoming, h), 1, 1)) * inv
         g = head_slice(gate, h).astype(F32)
         up = head_slice(cot, h).astype(F32)
         sig = 1.0 / (1.0 + jnp.exp(-g))
         act = g * sig
-        ga = up * act
-        gd = -jnp.sum(ga * att, 1, keepdims=True) * inv
-        ng = (ga * inv).astype(BF16)
+        gd = -jnp.sum(up * act * att, 1, keepdims=True) * inv
+        gd_ref[h] = gd
         outs.append((att * act).astype(BF16))
         ggates.append((up * att * sig * (1.0 + g * (1.0 - sig))).astype(BF16))
-        states.append(mm(ng, phi16, 0, 0))
         norms.append(jnp.sum(gd * phi, 0, keepdims=True))
-        dw = mm(ng, v, 1, 1) + gd
-        ds = (jnp.where(causal, dw * (1.0 + s), 0.0) * F**-0.5).astype(BF16)
-        dphi = mm(ng, state_h) + gd * norm_h
-        dq = dq + mm(ds, kh)
-        dq = dq + mm((dphi * two).astype(BF16), first_h, 1, 1)
-        dq = dq + mm((dphi * one * scale).astype(BF16), second_h, 1, 1)
-        dk = dk + mm(ds, qh, 0, 0)
-        dvs.append(mm(w16, ng, 0, 0))
     for p in range(H // 2):
         at = slice(2 * p * DV, 2 * (p + 1) * DV)
         out[:, at] = jnp.concatenate(outs[2 * p : 2 * p + 2], 1)
         ggate[:, at] = jnp.concatenate(ggates[2 * p : 2 * p + 2], 1)
+    return norm_block(norms)
+
+
+def query_part(
+    mixed, values, state, norm_rows, first, second, rows, s_ref, one_ref, two_ref, ng_ref, gd_ref,
+    dq_out, dk_out, dv_out,
+):
+    q, k, only = heads_of(mixed)
+    length = mixed.shape[0]
+    causal = causal_of(length)
+    incoming = state[...]
+    dq = jnp.zeros((length, H * F), F32)
+    dk = jnp.zeros((length, H * F), F32)
+    dvs = []
+    for h in range(H):
+        at = slice(h * FP, (h + 1) * FP)
+        s, ng, gd = s_ref[h], ng_ref[h], gd_ref[h]
+        one, two = one_ref[:, at], two_ref[:, at]
+        dw = mm(ng, head_slice(values, h), 1, 1) + gd
+        ds = (jnp.where(causal, dw * (1.0 + s), 0.0) * F**-0.5).astype(BF16)
+        dphi = mm(ng, head_state(incoming, h)) + gd * head_norm(norm_rows, h)
+        dq = dq + mm(ds, only(k, h))
+        dq = dq + mm((dphi * two).astype(BF16), first[:, at], 1, 1)
+        dq = dq + mm((dphi * one * rows[2:3, at]).astype(BF16), second[:, at], 1, 1)
+        dk = dk + mm(ds, only(q, h), 0, 0)
+        dvs.append(mm(weights_of(s, causal).astype(BF16), ng, 0, 0))
+    for p in range(H // 2):
+        at = slice(2 * p * DV, 2 * (p + 1) * DV)
         dv_out[:, at] = jnp.concatenate(dvs[2 * p : 2 * p + 2], 1)
-    store_state(state_out, states, norms)
     dq_out[...] = dq
     dk_out[...] = dk
 
 
-def value_part(mixed, values, state, dq_in, dk_in, dv_in, first, second, rows, gv, gm):
+def value_part(mixed, values, state, norm_rows, dq_in, dk_in, dv_in, first, second, rows, gv, gm):
     keys = mixed[:, H * F :].astype(BF16)
     incoming = state[...]
-    norm_rows = incoming[NORM_ROW : NORM_ROW + 16].astype(F32)
     dk = dk_in[...]
     dvs = []
     for h in range(H):
@@ -249,10 +292,12 @@
         )
 
     copy0().start()
+    yield
     copy0().wait_recv()
     both[...] = (state[part(core * half, half)].astype(F32) + theirs[...].astype(F32)).astype(BF16)
     each(half, lambda off: copy1(off).start())
     got[pair] = both[part(pair)]
+    yield
     each(half, lambda off: copy1(off).wait_recv())
 
     def add(i, total):
@@ -263,6 +308,7 @@
     lax.fori_loop(0, half, add, jnp.zeros(got.shape[1:], F32))
     each(half, lambda off: copy2(off).start())
     give[0, pair] = sums[pair]
+    yield
     late = core if not backward else 1 - core
     mine_late = late.astype(F32)
     other_late = 1.0 - mine_late
@@ -281,25 +327,27 @@
 
     hand_on(0)
     each(half, arrive)
+    yield
     each(half, lambda off: copy3(off).wait_recv(), 0)
-
-    def finish():
-        each(half, lambda off: copy3(off).wait_send(), 0)
-        each(half, lambda off: copy2(off).wait_send())
-        each(half, lambda off: copy1(off).wait_send())
-        copy0().wait_send()
-
-    return finish
+    yield
+    each(half, lambda off: copy3(off).wait_send(), 0)
+    each(half, lambda off: copy2(off).wait_send())
+    each(half, lambda off: copy1(off).wait_send())
+    copy0().wait_send()
+    yield
 
 
 def layer_kernel(n, *refs):
-    hidden, weight, conv, values, gate, cot, first, second, rows = refs[:9]
-    out, gh, gv, ggate, gw = refs[9:14]
-    proj, prev, later, mixed, state, before, grad_state, after = refs[14:22]
-    dq, dk, dv, gm, gp, hid, gps, part, got = refs[22:31]
-    scan1, scan2 = refs[31:36], refs[36:41]
-    sems1, sems2 = refs[41:49], refs[49:57]
-    sh, rh, halo, sa, ra, sb, rb, sc, rc, sd, rd, se, re = refs[57:]
+    sources, refs = refs[:9], refs[9:]
+    out, gh, gv, ggate, gw = refs[:5]
+    loaded, refs = refs[5:14], refs[14:]
+    hidden, weight, conv, values, gate, cot, first, second, rows = loaded
+    proj, prev, later, mixed, state, before, grad_state, after = refs[:8]
+    dq, dk, dv, gm, gp, hid, gps, part, got = refs[8:17]
+    s_ref, num_ref, one_ref, two_ref, ng_ref, inv_ref, gd_ref, norms1, norms2 = refs[17:26]
+    scan1, scan2 = refs[26:31], refs[31:36]
+    sems1, sems2 = refs[36:44], refs[44:52]
+    sh, rh, halo, sa, ra, sb, rb, sc, rc, sd, rd, se, re, load, sn1, rn1, sn2, rn2 = refs[52:]
     tables = (first, second, rows)
     length = hidden.shape[0]
 
@@ -374,9 +422,26 @@
         ref = gw.at[ident(*source), slot(off)]
         return remote(ref, ref, se.at[key, off], re.at[key, off], target)
 
+    def fetch(i):
+        return pltpu.make_async_copy(sources[i], loaded[i], load.at[i])
+
+    def copy_norm(ref, s, r, off):
+        return remote(ref.at[me], ref.at[me], s.at[off], r.at[off], (dp, lax.rem(me + off, n)))
+
+    def norm_total(ref, after_me):
+        def add(i, total):
+            use = i > me if after_me else i < me
+            return total + jnp.where(use, 1.0, 0.0) * ref[i]
+
+        return lax.fori_loop(0, n, add, jnp.zeros(ref.shape[1:], F32))
+
+    for i in range(9):
+        fetch(i).start()
     barrier = pltpu.get_barrier_semaphore()
     each(n, lambda off: greet((dp, lax.rem(me + off, n))))
     each(4, lambda i: greet((1 - dp, place * 4 + i)), 0)
+    fetch(0).wait()
+    fetch(1).wait()
     proj[...] = mm(hidden[...], weight[...]).astype(BF16)
     pl.semaphore_wait(barrier, n + 3)
 
@@ -386,6 +451,8 @@
 
     each(8, lambda off: copy_hid(off).start())
     hid[own] = hidden[:, columns(own)]
+    for i in range(2, 9):
+        fetch(i).wait()
 
     @pl.when(me > 0)
     def _():
@@ -396,11 +463,34 @@
         prev[...] = jnp.zeros(prev.shape, BF16)
 
     mix(proj, prev, conv, mixed)
-    key_part(mixed, values, *tables, state)
-    finish1 = scan_part(n, False, state, before, *scan1, *sems1)
-    query_part(mixed, values, gate, cot, before, *tables, out, ggate, grad_state, dq, dk, dv)
-    finish2 = scan_part(n, True, grad_state, after, *scan2, *sems2)
-    value_part(mixed, values, after, dq, dk, dv, *tables, gv, gm)
+    norms1[me] = key_part(mixed, values, *tables, state)
+    each(n, lambda off: copy_norm(norms1, sn1, rn1, off).start())
+    keys_scan = scan_part(n, False, state, before, *scan1, *sems1)
+    grad_scan = scan_part(n, True, grad_state, after, *scan2, *sems2)
+    next(keys_scan)
+    next(keys_scan)
+    local_part(mixed, values, *tables, s_ref, num_ref, one_ref, two_ref)
+    each(n, lambda off: copy_norm(norms1, sn1, rn1, off).wait_recv())
+    norm_in = norm_total(norms1, False)
+    next(keys_scan)
+    denom_part(norm_in, gate, cot, s_ref, one_ref, two_ref, ng_ref, inv_ref, grad_state)
+    next(grad_scan)
+    next(keys_scan)
+    next(grad_scan)
+    next(keys_scan)
+    norms2[me] = attend_part(
+        gate, cot, before, num_ref, one_ref, two_ref, inv_ref, gd_ref, out, ggate
+    )
+    each(n, lambda off: copy_norm(norms2, sn2, rn2, off).start())
+    next(grad_scan)
+    query_part(
+        mixed, values, before, norm_in, *tables, s_ref, one_ref, two_ref, ng_ref, gd_ref, dq, dk, dv
+    )
+    next(grad_scan)
+    each(n, lambda off: copy_norm(norms2, sn2, rn2, off).wait_recv())
+    norm_after = norm_total(norms2, True)
+    next(grad_scan)
+    value_part(mixed, values, after, norm_after, dq, dk, dv, *tables, gv, gm)
 
     @pl.when(me > 0)
     def _():
@@ -465,8 +555,10 @@
         if r:
             copy_gp(r).wait_send()
         copy_gp_on(r).wait_send()
-    finish1()
-    finish2()
+    next(keys_scan)
+    next(grad_scan)
+    each(n, lambda off: copy_norm(norms1, sn1, rn1, off).wait_send())
+    each(n, lambda off: copy_norm(norms2, sn2, rn2, off).wait_send())
     each(8, lambda off: copy_hid(off).wait_send())
 
     @pl.when(me < n - 1)
@@ -476,6 +568,14 @@
     @pl.when(me > 0)
     def _():
         copy_later().wait_send()
+
+
+def write_kernel(*refs):
+    copies = [pltpu.make_async_copy(refs[i], refs[5 + i], refs[10].at[i]) for i in range(5)]
+    for copy in copies:
+        copy.start()
+    for copy in copies:
+        copy.wait()
 
 
 def body(n, hidden_in, qk_weight, conv_weight, values, gate_in, cotangent):
@@ -485,7 +585,7 @@
     wide = v.shape[1]
     first, second, rows = feature_tables()
     half, count = n // 2, n // 4
-    size = 16 * -(-(NORM_ROW + 16) // (16 * n))
+    size = 16 * -(-NORM_ROW // (16 * n))
     piece = depth // (8 * count)
     sem, vmem = pltpu.SemaphoreType.DMA, pltpu.VMEM
     state = vmem((n * size, 128), BF16)
@@ -499,29 +599,46 @@
         ((length, wide), BF16), ((length, depth), BF16), ((length, wide), BF16),
         ((length, wide), BF16), ((8, count, piece, cols), BF16),
     ]
-    out, gh, gv, ggate, gw = pl.pallas_call(
+    args = [
+        tokens, qk_weight, conv_weight, v, gate, cot,
+        jnp.asarray(first, BF16), jnp.asarray(second, BF16), jnp.asarray(rows),
+    ]
+    results = pl.pallas_call(
         functools.partial(layer_kernel, n),
         out_shape=[jax.ShapeDtypeStruct(s, t) for s, t in outs],
-        in_specs=[VM] * 9,
+        in_specs=[pl.BlockSpec(memory_space=pl.ANY)] * 9,
         out_specs=[VM] * 5,
-        scratch_shapes=[
+        scratch_shapes=[vmem(x.shape, x.dtype) for x in args]
+        + [
             vmem((length, cols), BF16), vmem((16, cols), BF16), vmem((8, cols), F32),
             vmem((length, cols), F32), state, state, state, state,
             vmem((length, cols // 2), F32), vmem((length, cols // 2), F32),
             vmem((length, wide), F32), vmem((length, cols), F32), vmem((length, cols), BF16),
             vmem((8, length, depth // 8), BF16), vmem((8, length, cols), BF16),
             vmem((count, piece, cols), BF16), vmem((count, piece, cols), BF16),
+            vmem((H, length, length), F32), vmem((H, length, DV), F32),
+            vmem((length, H * FP), F32), vmem((length, H * FP), F32),
+            vmem((H, length, DV), BF16), vmem((H, length, 1), F32), vmem((H, length, 1), F32),
+            vmem((n, 16, 128), F32), vmem((n, 16, 128), F32),
         ]
         + scan * 2 + scan_sems * 2
-        + [sem((8,))] * 2 + [sem((4,))] * 5 + [sem((count,))] * 4 + [sem((7, count))] * 2,
+        + [sem((8,))] * 2 + [sem((4,))] * 5 + [sem((count,))] * 4 + [sem((7, count))] * 2
+        + [sem((9,))] + [sem((n,))] * 4,
         compiler_params=pltpu.CompilerParams(
-            vmem_limit_bytes=48 * 2**20, collective_id=0, has_side_effects=True
+            vmem_limit_bytes=60 * 2**20, collective_id=0, has_side_effects=True
         ),
-    )(
-        tokens, qk_weight, conv_weight, v, gate, cot,
-        jnp.asarray(first, BF16), jnp.asarray(second, BF16), jnp.asarray(rows),
-    )
-    return out[None], gh[None], gv[None], ggate[None], gw.reshape(depth, cols)
+    )(*args)
+    results = list(results)
+    results[4] = results[4].reshape(depth, cols)
+    out, gh, gv, ggate, gw = pl.pallas_call(
+        write_kernel,
+        out_shape=[jax.ShapeDtypeStruct(x.shape, x.dtype) for x in results],
+        in_specs=[pl.BlockSpec(memory_space=pl.ANY)] * 5,
+        out_specs=[pl.BlockSpec(memory_space=pl.ANY)] * 5,
+        scratch_shapes=[sem((5,))],
+        compiler_params=pltpu.CompilerParams(vmem_limit_bytes=60 * 2**20),
+    )(*results)
+    return out[None], gh[None], gv[None], ggate[None], gw
 
 
 def solution(mesh):

time: 80.8 us -> 126 us (1.56)
  Pallas kernels: 67.4 us -> 125 us
  local copies, waits for them, and re-layouts: 12.3 us -> 0 us
    pallas_call x0 -> x1, Pallas kernels: none -> 60.7 us  [body(): pl.pallas_call(write_kernel, out_shape=[jax.ShapeDtypeStruct(x.shape, x.d...]
    unnamed x23 -> x0, local copies, waits for them, and re-layouts: 12.3 us -> none
    pallas_call x1, Pallas kernels: 67.4 us -> 64.4 us  [body(): pl.pallas_call(functools.partial(layer_kernel, n), out_shape=[jax.ShapeDt...]
where the time goes in v5:
time: 126 us
  Pallas kernels  125 us (99%)
    pallas_call x1, Pallas kernels, body(): pl.pallas_call(functools.partial(layer_kernel, n), out_shape=[jax.ShapeDt...  64.4 us
    pallas_call x1, Pallas kernels, body(): pl.pallas_call(write_kernel, out_shape=[jax.ShapeDtypeStruct(x.shape, x.d...  60.7 us

profile of v5, /device:TPU:0, one launch (start us, length us, event | category | flops | bytes accessed | tf_op | source)
XLA Modules:
  0.0 125.8 jit_solution(3610024495455432665)
XLA Ops:
  0.6 64.4 %shard_map.128 = (bf16[128,512]{1,0:T(8,128)(2,1)}, bf16[128,2048]{1,0:T(8,128)(2,1)}, bf16[128,512]{1,0:T(8,128)(2,1)}, bf16[128,512]{1,0:T(8,128)(2,1)}, bf16[8,4,64,256]{3,2,1,0:T(8,128)(2,1)}) custom-call(bf16[128,2048]{1,0:T(8,128)(2,1)} %bitcast.10, bf16[2048,256]{1,0:T(8,128)(2,1)} %refs_1_.1, f32[3,256]{1,0:T(4,128)} %refs_2_.1, ...), custom_call_target="tpu_custom_call" | custom-call | tf_op jit(solution)/shard_map/pallas_call | solution.py:606
  65.1 60.7 %shard_map.129 = (bf16[128,512]{1,0:T(8,128)(2,1)}, bf16[128,2048]{1,0:T(8,128)(2,1)}, bf16[128,512]{1,0:T(8,128)(2,1)}, bf16[128,512]{1,0:T(8,128)(2,1)}, bf16[2048,256]{1,0:T(8,128)(2,1)}) custom-call(bf16[128,512]{1,0:T(8,128)(2,1)} %get-tuple-element.15.refs_0_, bf16[128,2048]{1,0:T(8,128)(2,1)} %get-tuple-element.16.refs_1_, ...), custom_call_target="tpu_custom_call" | custom-call | tf_op jit(solution)/shard_map/pallas_call | solution.py:633

commit v6 on v5

--- a/solution.py
+++ b/solution.py
@@ -449,7 +449,6 @@
     def _():
         copy_prev().start()
 
-    each(8, lambda off: copy_hid(off).start())
     hid[own] = hidden[:, columns(own)]
     for i in range(2, 9):
         fetch(i).wait()
@@ -465,24 +464,31 @@
     mix(proj, prev, conv, mixed)
     norms1[me] = key_part(mixed, values, *tables, state)
     each(n, lambda off: copy_norm(norms1, sn1, rn1, off).start())
+    copy_hid(1).start()
     keys_scan = scan_part(n, False, state, before, *scan1, *sems1)
     grad_scan = scan_part(n, True, grad_state, after, *scan2, *sems2)
     next(keys_scan)
     next(keys_scan)
+    copy_hid(2).start()
     local_part(mixed, values, *tables, s_ref, num_ref, one_ref, two_ref)
     each(n, lambda off: copy_norm(norms1, sn1, rn1, off).wait_recv())
     norm_in = norm_total(norms1, False)
     next(keys_scan)
+    copy_hid(3).start()
     denom_part(norm_in, gate, cot, s_ref, one_ref, two_ref, ng_ref, inv_ref, grad_state)
     next(grad_scan)
     next(keys_scan)
+    copy_hid(4).start()
     next(grad_scan)
+    copy_hid(5).start()
     next(keys_scan)
     norms2[me] = attend_part(
         gate, cot, before, num_ref, one_ref, two_ref, inv_ref, gd_ref, out, ggate
     )
     each(n, lambda off: copy_norm(norms2, sn2, rn2, off).start())
     next(grad_scan)
+    copy_hid(6).start()
+    copy_hid(7).start()
     query_part(
         mixed, values, before, norm_in, *tables, s_ref, one_ref, two_ref, ng_ref, gd_ref, dq, dk, dv
     )
@@ -571,11 +577,16 @@
 
 
 def write_kernel(*refs):
-    copies = [pltpu.make_async_copy(refs[i], refs[5 + i], refs[10].at[i]) for i in range(5)]
-    for copy in copies:
-        copy.start()
-    for copy in copies:
-        copy.wait()
+    sources, outs, held, loads, stores = refs[:5], refs[5:10], refs[10:15], refs[15], refs[16]
+    reads = [pltpu.make_async_copy(sources[i], held[i], loads.at[i]) for i in range(5)]
+    writes = [pltpu.make_async_copy(held[i], outs[i], stores.at[i]) for i in range(5)]
+    for read in reads:
+        read.start()
+    for read, write in zip(reads, writes):
+        read.wait()
+        write.start()
+    for write in writes:
+        write.wait()
 
 
 def body(n, hidden_in, qk_weight, conv_weight, values, gate_in, cotangent):
@@ -635,7 +646,7 @@
         out_shape=[jax.ShapeDtypeStruct(x.shape, x.dtype) for x in results],
         in_specs=[pl.BlockSpec(memory_space=pl.ANY)] * 5,
         out_specs=[pl.BlockSpec(memory_space=pl.ANY)] * 5,
-        scratch_shapes=[sem((5,))],
+        scratch_shapes=[vmem(x.shape, x.dtype) for x in results] + [sem((5,))] * 2,
         compiler_params=pltpu.CompilerParams(vmem_limit_bytes=60 * 2**20),
     )(*results)
     return out[None], gh[None], gv[None], ggate[None], gw

time: 126 us -> 68.8 us (0.55)
  Pallas kernels: 125 us -> 68 us
    pallas_call x1, Pallas kernels: 60.7 us -> 2.6 us  [body(): pl.pallas_call(write_kernel, out_shape=[jax.ShapeDtypeStruct(x.shape, x.d...]
where the time goes in v6:
time: 68.8 us; the launch traced here: 68.6 us
  Pallas kernels  68 us (99%)
    pallas_call x1, Pallas kernels, body(): pl.pallas_call(functools.partial(layer_kernel, n), out_shape=[jax.ShapeDt...  65.4 us
    pallas_call x1, Pallas kernels, body(): pl.pallas_call(write_kernel, out_shape=[jax.ShapeDtypeStruct(x.shape, x.d...  2.6 us

profile of v6, /device:TPU:0, one launch (start us, length us, event | category | flops | bytes accessed | tf_op | source)
XLA Modules:
  0.0 68.6 jit_solution(12272179945055720128)
XLA Ops:
  0.6 65.4 %shard_map.128 = (bf16[128,512]{1,0:T(8,128)(2,1)}, bf16[128,2048]{1,0:T(8,128)(2,1)}, bf16[128,512]{1,0:T(8,128)(2,1)}, bf16[128,512]{1,0:T(8,128)(2,1)}, bf16[8,4,64,256]{3,2,1,0:T(8,128)(2,1)}) custom-call(bf16[128,2048]{1,0:T(8,128)(2,1)} %bitcast.10, bf16[2048,256]{1,0:T(8,128)(2,1)} %refs_1_.1, f32[3,256]{1,0:T(4,128)} %refs_2_.1, ...), custom_call_target="tpu_custom_call" | custom-call | tf_op jit(solution)/shard_map/pallas_call | solution.py:617
  66.0 2.6 %shard_map.129 = (bf16[128,512]{1,0:T(8,128)(2,1)}, bf16[128,2048]{1,0:T(8,128)(2,1)}, bf16[128,512]{1,0:T(8,128)(2,1)}, bf16[128,512]{1,0:T(8,128)(2,1)}, bf16[2048,256]{1,0:T(8,128)(2,1)}) custom-call(bf16[128,512]{1,0:T(8,128)(2,1)} %get-tuple-element.15.refs_0_, bf16[128,2048]{1,0:T(8,128)(2,1)} %get-tuple-element.16.refs_1_, ...), custom_call_target="tpu_custom_call" | custom-call | tf_op jit(solution)/shard_map/pallas_call | solution.py:644
